TPU v7x, 512 devices: a whole 4x4x16 slice. The times are simulated.
512 devices in a mesh: lon: 64 (over z, y_hi, core), lat: 8 (over x, y_lo).
Axes of the slice: x: 4, y: 4 (y_hi: 2, y_lo: 2; y = y_hi * 2 + y_lo), z: 16, core: 2. Of those that a mesh axis runs over, the one named last changes fastest.
Arguments:
- tokens: bfloat16 [1536, 288, 512], P('lon', 'lat'), may hold values from -24 to 24
- norm_gain: float32 [512], replicated, may hold values from 0.1 to 1.9
- w_qkv: bfloat16 [512, 1536], replicated, may hold values from -1.767767 to 1.767767
- w_out: bfloat16 [512, 512], replicated, may hold values from -0.25 to 0.25
- pole_mask: int32 [288], replicated, may hold values from 0 to 1, as said below
Outputs:
- mixed: bfloat16 [1536, 288, 512], P('lon', 'lat')
Inputs may be any that keep to these rules, and one draw needn't show every extreme that they name: `pole_mask`: the first t and the last s rows are 0 and all others 1, with t and s between 1 and 5.
All inputs are finite; a program needn't handle non-finite values.
Results may differ from a plain program's by a relative error of at most 0.012.
The roundings to bfloat16 on the way count: a program that leaves them out, or rounds other values in their place, can miss the bound.
Values may be sent and summed in bfloat16 or wider, within the bound.
No kernel may reach another device: no remote copies, remote signals or barrier semaphores. Data moves between devices by JAX's collectives and lax.ppermute only.
A program may use at most 64 MiB of HBM per device.

v0:
```python
import jax
import jax.numpy as jnp
from jax import lax
from jax.sharding import PartitionSpec as P

HEADS = 8
WINDOW = 12
SHIFT = 6


EPS = 1e-05


def with_halo(x, sides, width, wrap):
    for axis, dim in sides:
        peers, length = (lax.axis_size(axis), x.shape[dim])
        up = [(i, (i + 1) % peers) for i in range(peers if wrap else peers - 1)]
        down = [(j, i) for i, j in up]
        last = lax.slice_in_dim(x, length - width, length, axis=dim)
        first = lax.slice_in_dim(x, 0, width, axis=dim)
        before = lax.ppermute(last, axis, up)
        after = lax.ppermute(first, axis, down)
        x = jnp.concatenate([before, x, after], axis=dim)
    return x


def layer_norm(tokens, norm_gain):
    values32 = tokens.astype(jnp.float32)
    average = jnp.mean(values32, axis=-1, keepdims=True)
    centred = values32 - average
    variance = jnp.mean(centred * centred, axis=-1, keepdims=True)
    return (centred * lax.rsqrt(variance + EPS) * norm_gain).astype(jnp.bfloat16)


def window_attend(queries, key_part, value_part, key_usable):
    head_size = queries.shape[-1]
    scores = jnp.einsum("nqhd,nkhd->nhqk", queries, key_part, preferred_element_type=jnp.float32)
    scores = scores * head_size ** (-0.5)
    scores = jnp.where(key_usable[:, None, None, :], scores, -1e30)
    row_max = jnp.max(scores, axis=-1, keepdims=True)
    exp_scores = jnp.exp(scores - row_max)
    probabilities = (exp_scores / jnp.sum(exp_scores, axis=-1, keepdims=True)).astype(jnp.bfloat16)
    context = jnp.einsum(
        "nhqk,nkhd->nqhd", probabilities, value_part, preferred_element_type=jnp.float32
    )
    return context.astype(jnp.bfloat16)


def to_windows(field):
    lon_ext, lat_ext, columns = field.shape
    field = field.reshape(lon_ext // WINDOW, WINDOW, lat_ext // WINDOW, WINDOW, columns)
    field = jnp.transpose(field, (0, 2, 1, 3, 4))
    return field.reshape(lon_ext // WINDOW, lat_ext // WINDOW, WINDOW * WINDOW, columns)


def from_windows(field, lon_ext, lat_ext):
    columns = field.shape[-1]
    field = field.reshape(lon_ext // WINDOW, lat_ext // WINDOW, WINDOW, WINDOW, columns)
    field = jnp.transpose(field, (0, 2, 1, 3, 4))
    return field.reshape(lon_ext, lat_ext, columns)


def attend_all(query_ext, keys_values, usable_rows):
    lon_ext, lat_ext, width = query_ext.shape
    head_size = width // HEADS
    lat_windows = lat_ext // WINDOW
    query_win = to_windows(query_ext)
    pair_win = to_windows(keys_values)
    key_usable = jnp.broadcast_to(
        usable_rows.reshape(lat_windows, 1, WINDOW), (lat_windows, WINDOW, WINDOW)
    )
    key_usable = key_usable.reshape(lat_windows, WINDOW * WINDOW)

    def attend_band(operands):
        query_rows, pair_rows = operands
        queries = query_rows.reshape(lat_windows, WINDOW * WINDOW, HEADS, head_size)
        key_part = pair_rows[:, :, :width].reshape(lat_windows, WINDOW * WINDOW, HEADS, head_size)
        value_part = pair_rows[:, :, width:].reshape(lat_windows, WINDOW * WINDOW, HEADS, head_size)
        context = window_attend(queries, key_part, value_part, key_usable)
        return context.reshape(lat_windows, WINDOW * WINDOW, width)

    context_win = lax.map(attend_band, (query_win, pair_win))
    return from_windows(context_win, lon_ext, lat_ext)


def shards(tokens, norm_gain, w_qkv, w_out, pole_mask):
    lon_dev, lat_dev, width = tokens.shape
    lat_ext = lat_dev + 2 * SHIFT
    normed = layer_norm(tokens, norm_gain)
    flattened = normed.reshape(-1, width)
    padded_mask = jnp.pad(pole_mask == 1, (SHIFT, SHIFT))
    band_start = lax.axis_index("lat") * lat_dev
    usable_rows = lax.dynamic_slice_in_dim(padded_mask, band_start, lat_ext, 0)
    projected = jnp.dot(flattened, w_qkv, preferred_element_type=jnp.float32).astype(jnp.bfloat16)
    projected = projected.reshape(lon_dev, lat_dev, 3 * width)
    local_queries = projected[:, :, :width]
    keys_values = with_halo(projected[:, :, width:], (("lon", 0),), SHIFT, True)
    keys_values = with_halo(keys_values, (("lat", 1),), SHIFT, False)
    query_ext = jnp.pad(local_queries, ((SHIFT, SHIFT), (SHIFT, SHIFT), (0, 0)))
    context_all = attend_all(query_ext, keys_values, usable_rows)
    context = context_all[SHIFT : SHIFT + lon_dev, SHIFT : SHIFT + lat_dev]
    update = jnp.dot(context.reshape(-1, width), w_out, preferred_element_type=jnp.float32)
    mixed = tokens.reshape(-1, width).astype(jnp.float32) + update
    return mixed.reshape(lon_dev, lat_dev, width).astype(jnp.bfloat16)


def solution(mesh):
    in_specs = (P("lon", "lat", None), P(), P(), P(), P())
    out_specs = P("lon", "lat", None)
    return jax.shard_map(shards, mesh=mesh, in_specs=in_specs, out_specs=out_specs, check_vma=False)
```

profile of v0, /device:TPU:2, one launch (start us, length us, event | category | flops | bytes accessed | tf_op | source)
XLA Modules:
  0.0 160.0 jit_solution(9589214382995622478)
XLA Ops:
  4.7 3.1 %convolution_convert_fusion = bf16[864,1536]{1,0:T(8,128)(2,1)} fusion(bf16[864,512]{1,0:T(8,128)(2,1)S(1)} %reshape.62, bf16[512,1536]{1,0:T(8,128)(2,1)S(1)} %copy-done), kind=kOutput, calls=%fused_computation.18 | convolution fusion | flops 1360281600 | bytes 5111808 | tf_op jit(solution)/shard_map/dot_general | solution.py:94
  7.8 4.2 %reshape.63 = bf16[24,36,1536]{2,1,0:T(8,128)(2,1)} reshape(bf16[864,1536]{1,0:T(8,128)(2,1)} %convolution_convert_fusion) | data formatting | bytes 5308416 | tf_op jit(solution)/shard_map/reshape | solution.py:95
  15.2 13.5 %collective-permute-start.1 = (bf16[6,36,1024]{2,1,0:T(8,128)(2,1)S(1)}, bf16[6,36,1024]{2,1,0:T(8,128)(2,1)S(1)}, u32[]{:S(2)}, u32[]{:S(2)}) collective-permute-start(bf16[6,36,1024]{2,1,0:T(8,128)(2,1)S(1)} %get-tuple-element.73), channel_id=1, source_target_pairs={{8,0},{16,8},{24,16},{32,24},{40,32},{48,40},{56,48},{64,56},{72,6... | collective-permute-start | bytes 1327112 | tf_op jit(solution)/shard_map/ppermute | solution.py:22
  30.4 3.0 %collective-permute-done = bf16[6,36,1024]{2,1,0:T(8,128)(2,1)S(1)} collective-permute-done((bf16[6,36,1024]{2,1,0:T(8,128)(2,1)S(1)}, bf16[6,36,1024]{2,1,0:T(8,128)(2,1)S(1)}, u32[]{:S(2)}, u32[]{:S(2)}) %collective-permute-start) | collective-permute-done | bytes 442400 | tf_op jit(solution)/shard_map/ppermute | solution.py:21
  36.8 2.6 %collective-permute-start.2 = (bf16[36,6,1024]{2,0,1:T(8,128)(2,1)}, bf16[36,6,1024]{2,0,1:T(8,128)(2,1)}, u32[]{:S(2)}, u32[]{:S(2)}) collective-permute-start(bf16[36,6,1024]{2,0,1:T(8,128)(2,1)} %copy.24), channel_id=1, source_target_pairs={{0,1},{1,2},{2,3},{3,4},{4,5},{5,6},{6,7},{8,9},{9,10},{10,11},{11... | collective-permute-start | bytes 1327112 | tf_op jit(solution)/shard_map/ppermute | solution.py:21
  40.5 4.3 %collective-permute-start.3 = (bf16[36,6,1024]{2,0,1:T(8,128)(2,1)}, bf16[36,6,1024]{2,0,1:T(8,128)(2,1)}, u32[]{:S(2)}, u32[]{:S(2)}) collective-permute-start(bf16[36,6,1024]{2,0,1:T(8,128)(2,1)} %copy.25), channel_id=1, source_target_pairs={{1,0},{2,1},{3,2},{4,3},{5,4},{6,5},{7,6},{9,8},{10,9},{11,10},{12... | collective-permute-start | bytes 1327112 | tf_op jit(solution)/shard_map/ppermute | solution.py:22
  44.8 2.2 %slice.43 = bf16[24,36,512]{2,1,0:T(8,128)(2,1)} slice(bf16[24,36,1536]{2,1,0:T(8,128)(2,1)} %reshape.63), slice={[0:24], [0:36], [0:512]} | slice | bytes 1769472 | tf_op jit(solution)/shard_map/slice | solution.py:96
  47.0 2.7 %copy.22 = f32[24,36,512]{2,1,0:T(8,128)} copy(bf16[24,36,512]{2,0,1:T(8,128)(2,1)} %param.7) | data formatting | bytes 2654208 | tf_op jit(solution)/shard_map/convert_element_type | solution.py:103
  50.0 3.0 %pad.9 = bf16[36,48,512]{2,1,0:T(8,128)(2,1)} pad(bf16[24,36,512]{2,1,0:T(8,128)(2,1)} %slice.43, bf16[]{:T(256)} %constant.14.clone.1), padding=6_6x6_6x0_0 | pad | bytes 2654210 | tf_op jit(solution)/shard_map/jit(_pad)/pad | solution.py:99
  53.0 3.9 %reshape.66 = bf16[3,12,4,12,512]{4,3,2,1,0:T(8,128)(2,1)} reshape(bf16[36,48,512]{2,1,0:T(8,128)(2,1)} %pad.9) | data formatting | bytes 3538944 | tf_op jit(solution)/shard_map/reshape | solution.py:51
  56.9 4.5 %copy.29 = bf16[3,4,12,12,512]{4,1,3,2,0:T(4,128)(2,1)} copy(bf16[3,4,12,12,512]{4,3,1,2,0:T(8,128)(2,1)} %bitcast.47) | data formatting | bytes 3538944 | tf_op jit(solution)/shard_map/transpose | solution.py:52
  61.4 2.7 %reshape.71 = f32[864,512]{1,0:T(8,128)} reshape(f32[24,36,512]{2,1,0:T(8,128)} %copy.22) | data formatting | bytes 3538944 | tf_op jit(solution)/shard_map/convert_element_type | solution.py:103
  66.8 3.5 %pad_maximum_fusion = bf16[36,48,1024]{2,1,0:T(8,128)(2,1)} fusion(bf16[36,6,1024]{2,1,0:T(8,128)(2,1)S(1)} %copy.27, bf16[6,36,1024]{2,1,0:T(8,128)(2,1)S(1)} %copy-done.6, bf16[24,36,1024]{2,1,0:T(8,128)(2,1)S(1)} %slice.41, bf16[6,36,1024]{2,1,0:T(8,128)(2,1)S(1)} %copy-done.4, bf16[36,6,1024]{2,1,0:T(8,128)(2,1)S(1)} %copy.26), kind=kLoop, calls=%fused_computation.17 | loop fusion | flops 17694720 | bytes 7077888 | tf_op jit(solution)/shard_map/concatenate | solution.py:23
  70.2 6.6 %reshape.64 = bf16[3,12,4,12,1024]{4,3,2,1,0:T(8,128)(2,1)} reshape(bf16[36,48,1024]{2,1,0:T(8,128)(2,1)} %pad_maximum_fusion) | data formatting | bytes 7077888 | tf_op jit(solution)/shard_map/reshape | solution.py:51
  76.8 7.5 %copy.28 = bf16[3,4,12,12,1024]{4,1,3,2,0:T(4,128)(2,1)} copy(bf16[3,4,12,12,1024]{4,3,1,2,0:T(8,128)(2,1)} %bitcast.45) | data formatting | bytes 7077888 | tf_op jit(solution)/shard_map/transpose | solution.py:52
  84.3 58.2 %while.11 = (s32[]{:T(128)}, bf16[3,4,144,512]{3,1,2,0:T(4,128)(2,1)}, bf16[3,4,144,1024]{3,1,2,0:T(4,128)(2,1)}, bf16[3,4,144,512]{3,1,2,0:T(4,128)(2,1)}, pred[4,12]{1,0:T(4,128)(4,1)S(1)}, /*index=5*/s32[]{:T(128)}) while((s32[]{:T(128)}, bf16[3,4,144,512]{3,1,2,0:T(4,128)(2,1)}, bf16[3,4,144,1024]{3,1,2,0:T(4,128)(2,1)}, ...), condition=%wide.region_5.6_spmd.clone, body=%wide.region_2.5_spmd.clone.sunk | while | flops 174145680 | bytes 19503996 | solution.py:82
  86.0 2.5 %copy.44 = bf16[1,4,144,1024]{2,3,1,0:T(8,128)(2,1)} copy(bf16[1,4,144,1024]{3,1,2,0:T(4,128)(2,1)S(1)} %constant_dynamic-slice_fusion.4) | data formatting | bytes 2359296 | tf_op jit(solution)/shard_map/while/body/jit(dynamic_index_in_dim)/dynamic_slice | solution.py:82
  88.4 3.0 %fusion.34 = (bf16[4,144,512]{1,2,0:T(8,128)(2,1)}, bf16[4,144,512]{1,2,0:T(8,128)(2,1)}) fusion(bf16[4,144,1024]{1,2,0:T(8,128)(2,1)} %bitcast.39), kind=kLoop, calls=%fused_computation.30.clone.1 | loop fusion | bytes 2359296 | tf_op jit(solution)/shard_map/while/body/eval_jaxpr/slice | solution.py:77
  93.4 5.4 %fusion.35 = (f32[4,8,144]{2,1,0:T(8,128)S(1)}, f32[4,8,144,144]{2,3,1,0:T(8,128)}) fusion(pred[4,144]{1,0:T(4,128)(4,1)S(1)} %broadcast_in_dim.65, bf16[4,144,8,64]{1,3,2,0:T(8,128)(2,1)S(1)} %bitcast.40, bf16[4,144,8,64]{1,3,2,0:T(8,128)(2,1)} %bitcast.43), kind=kOutput, calls=%fused_computation.31.clone.1 | convolution fusion | flops 87589008 | bytes 3852864 | tf_op jit(solution)/shard_map/while/body/eval_jaxpr/sub | solution.py:41
  98.8 3.2 %fusion.36 = bf16[4,8,64,144]{3,2,1,0:T(8,128)(2,1)S(1)} fusion(bf16[4,144,8,64]{1,3,2,0:T(8,128)(2,1)} %bitcast.42, f32[4,8,144,144]{2,3,1,0:T(8,128)} %get-tuple-element.111, f32[4,8,144]{2,1,0:T(8,128)S(1)} %get-tuple-element.112), kind=kOutput, calls=%fused_computation.10.clone.1 | convolution fusion | flops 86556672 | bytes 3852288 | tf_op jit(solution)/shard_map/while/body/eval_jaxpr/nhqk,nkhd->nqhd/dot_general | solution.py:43
  105.4 2.5 %copy.44 = bf16[1,4,144,1024]{2,3,1,0:T(8,128)(2,1)} copy(bf16[1,4,144,1024]{3,1,2,0:T(4,128)(2,1)S(1)} %constant_dynamic-slice_fusion.4) | data formatting | bytes 2359296 | tf_op jit(solution)/shard_map/while/body/jit(dynamic_index_in_dim)/dynamic_slice | solution.py:82
  107.8 3.0 %fusion.34 = (bf16[4,144,512]{1,2,0:T(8,128)(2,1)}, bf16[4,144,512]{1,2,0:T(8,128)(2,1)}) fusion(bf16[4,144,1024]{1,2,0:T(8,128)(2,1)} %bitcast.39), kind=kLoop, calls=%fused_computation.30.clone.1 | loop fusion | bytes 2359296 | tf_op jit(solution)/shard_map/while/body/eval_jaxpr/slice | solution.py:77
  112.8 5.4 %fusion.35 = (f32[4,8,144]{2,1,0:T(8,128)S(1)}, f32[4,8,144,144]{2,3,1,0:T(8,128)}) fusion(pred[4,144]{1,0:T(4,128)(4,1)S(1)} %broadcast_in_dim.65, bf16[4,144,8,64]{1,3,2,0:T(8,128)(2,1)S(1)} %bitcast.40, bf16[4,144,8,64]{1,3,2,0:T(8,128)(2,1)} %bitcast.43), kind=kOutput, calls=%fused_computation.31.clone.1 | convolution fusion | flops 87589008 | bytes 3852864 | tf_op jit(solution)/shard_map/while/body/eval_jaxpr/sub | solution.py:41
  118.2 3.2 %fusion.36 = bf16[4,8,64,144]{3,2,1,0:T(8,128)(2,1)S(1)} fusion(bf16[4,144,8,64]{1,3,2,0:T(8,128)(2,1)} %bitcast.42, f32[4,8,144,144]{2,3,1,0:T(8,128)} %get-tuple-element.111, f32[4,8,144]{2,1,0:T(8,128)S(1)} %get-tuple-element.112), kind=kOutput, calls=%fused_computation.10.clone.1 | convolution fusion | flops 86556672 | bytes 3852288 | tf_op jit(solution)/shard_map/while/body/eval_jaxpr/nhqk,nkhd->nqhd/dot_general | solution.py:43
  124.8 2.5 %copy.44 = bf16[1,4,144,1024]{2,3,1,0:T(8,128)(2,1)} copy(bf16[1,4,144,1024]{3,1,2,0:T(4,128)(2,1)S(1)} %constant_dynamic-slice_fusion.4) | data formatting | bytes 2359296 | tf_op jit(solution)/shard_map/while/body/jit(dynamic_index_in_dim)/dynamic_slice | solution.py:82
  127.2 3.0 %fusion.34 = (bf16[4,144,512]{1,2,0:T(8,128)(2,1)}, bf16[4,144,512]{1,2,0:T(8,128)(2,1)}) fusion(bf16[4,144,1024]{1,2,0:T(8,128)(2,1)} %bitcast.39), kind=kLoop, calls=%fused_computation.30.clone.1 | loop fusion | bytes 2359296 | tf_op jit(solution)/shard_map/while/body/eval_jaxpr/slice | solution.py:77
  132.2 5.3 %fusion.35 = (f32[4,8,144]{2,1,0:T(8,128)S(1)}, f32[4,8,144,144]{2,3,1,0:T(8,128)}) fusion(pred[4,144]{1,0:T(4,128)(4,1)S(1)} %broadcast_in_dim.65, bf16[4,144,8,64]{1,3,2,0:T(8,128)(2,1)S(1)} %bitcast.40, bf16[4,144,8,64]{1,3,2,0:T(8,128)(2,1)} %bitcast.43), kind=kOutput, calls=%fused_computation.31.clone.1 | convolution fusion | flops 87589008 | bytes 3852864 | tf_op jit(solution)/shard_map/while/body/eval_jaxpr/sub | solution.py:41
  137.6 3.2 %fusion.36 = bf16[4,8,64,144]{3,2,1,0:T(8,128)(2,1)S(1)} fusion(bf16[4,144,8,64]{1,3,2,0:T(8,128)(2,1)} %bitcast.42, f32[4,8,144,144]{2,3,1,0:T(8,128)} %get-tuple-element.111, f32[4,8,144]{2,1,0:T(8,128)S(1)} %get-tuple-element.112), kind=kOutput, calls=%fused_computation.10.clone.1 | convolution fusion | flops 86556672 | bytes 3852288 | tf_op jit(solution)/shard_map/while/body/eval_jaxpr/nhqk,nkhd->nqhd/dot_general | solution.py:43
  142.5 3.5 %copy.33 = bf16[3,12,4,12,512]{4,3,2,1,0:T(8,128)(2,1)} copy(bf16[3,12,4,12,512]{4,2,3,1,0:T(4,128)(2,1)} %bitcast.48) | data formatting | bytes 3538944 | tf_op jit(solution)/shard_map/transpose | solution.py:59
  146.0 3.9 %reshape.69 = bf16[36,48,512]{2,1,0:T(8,128)(2,1)} reshape(bf16[3,12,4,12,512]{4,3,2,1,0:T(8,128)(2,1)} %copy.33) | data formatting | bytes 3538944 | tf_op jit(solution)/shard_map/reshape | solution.py:60
  149.9 2.8 %slice.44 = bf16[24,36,512]{2,1,0:T(8,128)(2,1)} slice(bf16[36,48,512]{2,1,0:T(8,128)(2,1)} %reshape.69), slice={[6:30], [6:42], [0:512]} | slice | bytes 1769472 | tf_op jit(solution)/shard_map/slice | solution.py:101
  154.8 2.9 %add_convert_fusion = bf16[864,512]{1,0:T(8,128)(2,1)} fusion(f32[864,512]{1,0:T(8,128)S(1)} %copy-done.2, bf16[864,512]{1,0:T(8,128)(2,1)} %reshape.70, bf16[512,512]{1,0:T(8,128)(2,1)} %param.10), kind=kOutput, calls=%fused_computation.19 | convolution fusion | flops 453869568 | bytes 4063232 | tf_op jit(solution)/shard_map/dot_general | solution.py:102
  (62 shorter events, 37.5 us)
Async XLA Ops:
  0.0 4.7 %copy-start = (bf16[512,1536]{1,0:T(8,128)(2,1)S(1)}, bf16[512,1536]{1,0:T(8,128)(2,1)}, u32[]{:S(2)}) copy-start(bf16[512,1536]{1,0:T(8,128)(2,1)} %param.9) | copy-start | bytes 4718596
  0.0 3.2 %copy-start.1 = (bf16[24,36,512]{2,0,1:T(8,128)(2,1)S(1)}, bf16[24,36,512]{2,0,1:T(8,128)(2,1)}, u32[]{:S(2)}) copy-start(bf16[24,36,512]{2,0,1:T(8,128)(2,1)} %param.7) | copy-start | bytes 2654212
  13.3 20.1 %collective-permute-start = (bf16[6,36,1024]{2,1,0:T(8,128)(2,1)S(1)}, bf16[6,36,1024]{2,1,0:T(8,128)(2,1)S(1)}, u32[]{:S(2)}, u32[]{:S(2)}) collective-permute-start(bf16[6,36,1024]{2,1,0:T(8,128)(2,1)S(1)} %get-tuple-element.72), channel_id=1, source_target_pairs={{0,8},{8,16},{16,24},{24,32},{32,40},{40,48},{48,56},{56,64},{64,7... | collective-permute-start | bytes 1327112 | tf_op jit(solution)/shard_map/ppermute | solution.py:21
  15.2 19.9 %collective-permute-start.1 = (bf16[6,36,1024]{2,1,0:T(8,128)(2,1)S(1)}, bf16[6,36,1024]{2,1,0:T(8,128)(2,1)S(1)}, u32[]{:S(2)}, u32[]{:S(2)}) collective-permute-start(bf16[6,36,1024]{2,1,0:T(8,128)(2,1)S(1)} %get-tuple-element.73), channel_id=1, source_target_pairs={{8,0},{16,8},{24,16},{32,24},{40,32},{48,40},{56,48},{64,56},{72,6... | collective-permute-start | bytes 1327112 | tf_op jit(solution)/shard_map/ppermute | solution.py:22
  33.3 2.0 %copy-start.3 = (bf16[6,36,1024]{2,1,0:T(8,128)(2,1)}, bf16[6,36,1024]{2,1,0:T(8,128)(2,1)S(1)}, u32[]{:S(2)}) copy-start(bf16[6,36,1024]{2,1,0:T(8,128)(2,1)S(1)} %collective-permute-done) | copy-start | bytes 1327108
  35.0 0.8 copy-start.5
  36.8 27.2 %collective-permute-start.2 = (bf16[36,6,1024]{2,0,1:T(8,128)(2,1)}, bf16[36,6,1024]{2,0,1:T(8,128)(2,1)}, u32[]{:S(2)}, u32[]{:S(2)}) collective-permute-start(bf16[36,6,1024]{2,0,1:T(8,128)(2,1)} %copy.24), channel_id=1, source_target_pairs={{0,1},{1,2},{2,3},{3,4},{4,5},{5,6},{6,7},{8,9},{9,10},{10,11},{11... | collective-permute-start | bytes 1327112 | tf_op jit(solution)/shard_map/ppermute | solution.py:21
  40.5 25.0 %collective-permute-start.3 = (bf16[36,6,1024]{2,0,1:T(8,128)(2,1)}, bf16[36,6,1024]{2,0,1:T(8,128)(2,1)}, u32[]{:S(2)}, u32[]{:S(2)}) collective-permute-start(bf16[36,6,1024]{2,0,1:T(8,128)(2,1)} %copy.25), channel_id=1, source_target_pairs={{1,0},{2,1},{3,2},{4,3},{5,4},{6,5},{7,6},{9,8},{10,9},{11,10},{12... | collective-permute-start | bytes 1327112 | tf_op jit(solution)/shard_map/ppermute | solution.py:22
  44.8 5.0 %copy-start.7 = (s32[288]{0:T(512)S(1)}, s32[288]{0:T(512)}, u32[]{:S(2)}) copy-start(s32[288]{0:T(512)} %param.11) | copy-start | bytes 3460
  64.1 2.7 %copy-start.4 = (bf16[6,36,1024]{2,1,0:T(8,128)(2,1)S(1)}, bf16[6,36,1024]{2,1,0:T(8,128)(2,1)}, u32[]{:S(2)}) copy-start(bf16[6,36,1024]{2,1,0:T(8,128)(2,1)} %copy-done.3) | copy-start | bytes 1327108
  64.1 2.7 %copy-start.6 = (bf16[6,36,1024]{2,1,0:T(8,128)(2,1)S(1)}, bf16[6,36,1024]{2,1,0:T(8,128)(2,1)}, u32[]{:S(2)}) copy-start(bf16[6,36,1024]{2,1,0:T(8,128)(2,1)} %copy-done.5) | copy-start | bytes 1327108
  149.9 4.9 %copy-start.2 = (f32[864,512]{1,0:T(8,128)S(1)}, f32[864,512]{1,0:T(8,128)}, u32[]{:S(2)}) copy-start(f32[864,512]{1,0:T(8,128)} %reshape.71) | copy-start | bytes 5308420
where the time goes:
time: 162 us; the launch traced here: 160 us
  local copies, waits for them, and re-layouts  93.3 us (58%)
  matrix products  31.5 us (19%)
  starting transfers between devices  22.3 us (14%)
  other arithmetic  7.92 us (5%)
  waiting for transfers between devices  4.66 us (3%)
    dynamic_slice x12, local copies, waits for them, and re-layouts, attend_all(): context_win = lax.map(attend_band, (query_win, pair_win))  18.1 us
    ppermute x2, starting transfers between devices, with_halo(): after = lax.ppermute(first, axis, down)  17.8 us
    sub x3, matrix products, window_attend(): exp_scores = jnp.exp(scores - row_max)  16.1 us
    transpose x2, local copies, waits for them, and re-layouts, to_windows(): field = jnp.transpose(field, (0, 2, 1, 3, 4))  12 us
    reshape x2, local copies, waits for them, and re-layouts, to_windows(): field.reshape(lon_ext // WINDOW, WINDOW, lat_ext // WINDOW, WINDOW, columns)  10.4 us
    dot_general x3, matrix products, window_attend(): jnp.einsum('nhqk,nkhd->nqhd', probabilities, value_part, preferred_elemen...  9.51 us
    slice x3, local copies, waits for them, and re-layouts, attend_band(): pair_rows[:, :, :width]  8.94 us
    convert_element_type x2, local copies, waits for them, and re-layouts, shards(): mixed = tokens.reshape(-1, width).astype(jnp.float32) + update  5.41 us
  transfers between devices with their start and end apart: 4, of which 2 were waited for; matrix products, arithmetic and copies ran while one was open for 15% of the time, Pallas kernels for 0%

commit v1 on v0

v1 whole, which is shorter than its diff:
```python
import functools

import jax
import jax.numpy as jnp
from jax import lax
from jax.experimental import pallas as pl
from jax.experimental.pallas import tpu as pltpu
from jax.sharding import PartitionSpec as P

WIDTH = 512
HEADS = 8
WINDOW = 12
SHIFT = 6
KEYS = WINDOW * WINDOW
EPS = 1e-05
LON = 24
LAT = 36
EDGE = LAT * SHIFT
BF = jnp.bfloat16
F32 = jnp.float32


def normalise(window_tokens, gain, normed, rows):
    block = 144
    for start in range(0, rows, block):
        values = window_tokens[start : start + block, :]
        average = jnp.sum(values, axis=-1, keepdims=True) * (1.0 / WIDTH)
        centred = values - average
        variance = jnp.sum(centred * centred, axis=-1, keepdims=True) * (1.0 / WIDTH)
        normed[start : start + block, :] = (centred * lax.rsqrt(variance + EPS) * gain).astype(BF)


def attend(window_tokens, gain_ref, w_qkv, w_out, counts, bias, normed, q_rows, pairs, queries, context, mixed):
    total = KEYS * len(counts)
    normalise(window_tokens, gain_ref[...], normed, total)
    offsets = []
    here = 0
    for index, count in enumerate(counts):
        offsets.append(here)
        q_rows[here : here + count, :] = normed[KEYS * index : KEYS * index + count, :]
        here += count
    asked = here
    for col in range(0, 2 * WIDTH, 256):
        part = jnp.dot(normed[...], w_qkv[:, WIDTH + col : WIDTH + col + 256], preferred_element_type=F32)
        pairs[:, col : col + 256] = part.astype(BF)
    for col in range(0, WIDTH, 256):
        part = jnp.dot(q_rows[...], w_qkv[:, col : col + 256], preferred_element_type=F32)
        queries[:, col : col + 256] = (part.astype(BF).astype(F32) * (WIDTH // HEADS) ** (-0.5)).astype(BF)
    lane = lax.broadcasted_iota(jnp.int32, (1, 128), 1)
    low32 = lane < 64
    keep_low = low32.astype(F32).astype(BF)
    keep_high = (lane >= 64).astype(F32).astype(BF)
    ones = jnp.ones((KEYS, 128), BF)
    for index, count in enumerate(counts):
        base, q_base = KEYS * index, offsets[index]
        for pair in range(HEADS // 2):
            cols = slice(128 * pair, 128 * pair + 128)
            both = queries[q_base : q_base + count, cols]
            stacked = jnp.concatenate([both * keep_low, both * keep_high], axis=0)
            key_part = pairs[base : base + KEYS, cols]
            value_part = pairs[base : base + KEYS, WIDTH + 128 * pair : WIDTH + 128 * pair + 128]
            scores = lax.dot_general(stacked, key_part, (((1,), (1,)), ((), ())), preferred_element_type=F32)
            if bias is not None:
                scores = scores + bias[index]
            row_max = jnp.max(scores, axis=-1, keepdims=True)
            exp_scores = jnp.exp(scores - row_max).astype(BF)
            widened = jnp.concatenate([value_part, ones], axis=1)
            summed = jnp.dot(exp_scores, widened, preferred_element_type=F32)
            first, second = summed[:count], summed[count:]
            top = jnp.where(low32, first[:, :128], second[:, :128])
            under = jnp.where(low32, first[:, 128:], second[:, 128:])
            context[q_base : q_base + count, cols] = (top / under).astype(BF)
    for col in range(0, WIDTH, 256):
        part = jnp.dot(context[...], w_out[:, col : col + 256], preferred_element_type=F32)
        for index, count in enumerate(counts):
            q_base = offsets[index]
            mixed[q_base : q_base + count, col : col + 256] = (
                part[q_base : q_base + count] + window_tokens[KEYS * index : KEYS * index + count, col : col + 256]
            )
    return offsets


def pack_lon(x, east, west, east32, west32):
    for lat in range(LAT):
        row = x[lat].astype(F32)
        west32[SHIFT * lat : SHIFT * lat + SHIFT, :] = row[0:SHIFT]
        east32[SHIFT * lat : SHIFT * lat + SHIFT, :] = row[LON - SHIFT : LON]
    west[...] = west32[...].astype(BF)
    east[...] = east32[...].astype(BF)


def pack_lat(x, from_west, from_east, north, south, work):
    own = SHIFT * LON
    for target, lat, halo in ((south, 0, 0), (north, LAT - SHIFT, EDGE - 36)):
        target[0:own, :] = x[lat : lat + SHIFT].reshape(own, WIDTH)
        work[0:36, :] = from_west[...].astype(F32)[halo : halo + 36]
        work[36:72, :] = from_east[...].astype(F32)[halo : halo + 36]
        target[own : own + 72, :] = work[...].astype(BF)


def middle(x, gain, w_qkv, w_out, out, x32, stack, normed, q_rows, pairs, queries, context, mixed):
    x32[...] = x[SHIFT : LAT - SHIFT].astype(F32)
    for lat in range(24):
        stack[12 * lat : 12 * lat + 12, :] = x32[lat, 6:18, :]
    attend(stack, gain, w_qkv, w_out, (144, 144), None, normed, q_rows, pairs, queries, context, mixed)
    for lat in range(24):
        x32[lat, 6:18, :] = mixed[12 * lat : 12 * lat + 12, :]
    out[...] = x32[...].astype(BF)


def sides(x, from_west, from_east, done, gain, w_qkv, w_out, out, x32, w32, e32, stack, normed, q_rows, pairs, queries, context, mixed):
    x32[...] = x[SHIFT : LAT - SHIFT].astype(F32)
    w32[...] = from_west[...].astype(F32)
    e32[...] = from_east[...].astype(F32)
    for index in range(4):
        band, east = index // 2, index % 2
        lon = 18 if east else 0
        base = KEYS * index
        for step in range(12):
            stack[base + 6 * step : base + 6 * step + 6, :] = x32[12 * band + step, lon : lon + 6, :]
        halo = e32 if east else w32
        stack[base + 72 : base + 144, :] = halo[36 + 72 * band : 108 + 72 * band, :]
    offsets = attend(stack, gain, w_qkv, w_out, (80,) * 4, None, normed, q_rows, pairs, queries, context, mixed)
    x32[...] = done[...].astype(F32)
    for index in range(4):
        band, east = index // 2, index % 2
        lon = 18 if east else 0
        for step in range(12):
            x32[12 * band + step, lon : lon + 6, :] = mixed[offsets[index] + 6 * step : offsets[index] + 6 * step + 6, :]
    out[...] = x32[...].astype(BF)


def poles(
    mask, x, from_west, from_east, from_south, from_north, done, gain, w_qkv, w_out, out,
    x32, w32, e32, s32, n32, stack, normed, q_rows, pairs, queries, context, mixed,
):
    x32[0:SHIFT] = x[0:SHIFT].astype(F32)
    x32[SHIFT : 2 * SHIFT] = x[LAT - SHIFT : LAT].astype(F32)
    w32[...] = from_west[...].astype(F32)
    e32[...] = from_east[...].astype(F32)
    s32[...] = from_south[...].astype(F32)
    n32[...] = from_north[...].astype(F32)
    band = lax.axis_index("lat")
    first = band * LAT
    key = lax.broadcasted_iota(jnp.int32, (1, KEYS), 1)
    in_halo = key >= 72
    inner = jnp.where(in_halo, key - 72, key)
    row_wide = inner // 12
    row_corner = jnp.where(inner >= 36, inner - 36, inner) // 6
    biases = []
    counts = []
    for north in range(2):
        halo = n32 if north else s32
        lat_at = first + LAT - SHIFT if north else first
        halo_at = first + LAT if north else first - SHIFT
        bias_wide = jnp.zeros((1, KEYS), F32)
        bias_corner = jnp.zeros((1, KEYS), F32)
        for step in range(SHIFT):
            own_ok = mask[lat_at + step] == 1
            there = halo_at + step
            exists = jnp.logical_and(there >= 0, there < 288)
            halo_ok = jnp.logical_and(exists, mask[jnp.clip(there, 0, 287)] == 1)
            own_bias = jnp.where(own_ok, 0.0, -1e30)
            halo_bias = jnp.where(halo_ok, 0.0, -1e30)
            step_bias = jnp.where(in_halo, halo_bias, own_bias)
            bias_wide = jnp.where(row_wide == step, step_bias, bias_wide)
            bias_corner = jnp.where(row_corner == step, step_bias, bias_corner)
        base = 3 * KEYS * north
        for step in range(SHIFT):
            row = x32[SHIFT * north + step]
            edge = halo[LON * step : LON * step + LON]
            stack[base + 12 * step : base + 12 * step + 12, :] = row[6:18]
            stack[base + 72 + 12 * step : base + 84 + 12 * step, :] = edge[6:18]
            stack[base + 144 + 6 * step : base + 150 + 6 * step, :] = row[0:6]
            stack[base + 216 + 6 * step : base + 222 + 6 * step, :] = edge[0:6]
            stack[base + 288 + 6 * step : base + 294 + 6 * step, :] = row[18:24]
            stack[base + 360 + 6 * step : base + 366 + 6 * step, :] = edge[18:24]
        at = EDGE - 36 if north else 0
        stack[base + 180 : base + 216, :] = w32[at : at + 36, :]
        stack[base + 252 : base + 288, :] = halo[144:180, :]
        stack[base + 324 : base + 360, :] = e32[at : at + 36, :]
        stack[base + 396 : base + 432, :] = halo[180:216, :]
        biases += [bias_wide, bias_corner, bias_corner]
        counts += [80, 48, 48]
    offsets = attend(stack, gain, w_qkv, w_out, tuple(counts), biases, normed, q_rows, pairs, queries, context, mixed)
    for north in range(2):
        wide, west, east = offsets[3 * north : 3 * north + 3]
        for step in range(SHIFT):
            at = SHIFT * north + step
            x32[at, 6:18, :] = mixed[wide + 12 * step : wide + 12 * step + 12, :]
            x32[at, 0:6, :] = mixed[west + 6 * step : west + 6 * step + 6, :]
            x32[at, 18:24, :] = mixed[east + 6 * step : east + 6 * step + 6, :]
    out[0:SHIFT] = x32[0:SHIFT].astype(BF)
    out[SHIFT : LAT - SHIFT] = done[...]
    out[LAT - SHIFT : LAT] = x32[SHIFT : 2 * SHIFT].astype(BF)


def work_space(counts):
    total, asked = KEYS * len(counts), sum(counts)
    return [
        pltpu.VMEM((total, WIDTH), F32),
        pltpu.VMEM((total, WIDTH), BF),
        pltpu.VMEM((asked, WIDTH), BF),
        pltpu.VMEM((total, 2 * WIDTH), BF),
        pltpu.VMEM((asked, WIDTH), BF),
        pltpu.VMEM((asked, WIDTH), BF),
        pltpu.VMEM((asked, WIDTH), F32),
    ]


def call(body, out_shape, scratch, flops, *operands, smem=0):
    vmem = pl.BlockSpec(memory_space=pltpu.VMEM)
    specs = [pl.BlockSpec(memory_space=pltpu.SMEM)] * smem + [vmem] * (len(operands) - smem)
    return pl.pallas_call(
        body,
        out_shape=out_shape,
        in_specs=specs,
        out_specs=jax.tree.map(lambda _: vmem, out_shape),
        scratch_shapes=scratch,
        compiler_params=pltpu.CompilerParams(vmem_limit_bytes=40 * 2**20),
        cost_estimate=pl.CostEstimate(flops=flops, bytes_accessed=4_000_000, transcendentals=0),
    )(*operands)


def shards(tokens, norm_gain, w_qkv, w_out, pole_mask):
    x = jnp.transpose(tokens, (1, 0, 2))
    gain = norm_gain.reshape(1, WIDTH)
    lons, lats = lax.axis_size("lon"), lax.axis_size("lat")
    eastward = [(i, (i + 1) % lons) for i in range(lons)]
    northward = [(i, i + 1) for i in range(lats - 1)]
    edge = jax.ShapeDtypeStruct((EDGE, WIDTH), BF)
    inner = jax.ShapeDtypeStruct((LAT - 2 * SHIFT, LON, WIDTH), BF)
    edge32 = pltpu.VMEM((EDGE, WIDTH), F32)
    inner32 = pltpu.VMEM((LAT - 2 * SHIFT, LON, WIDTH), F32)
    east, west = call(pack_lon, (edge, edge), [edge32, edge32], 1_000_000, x)
    from_west = lax.ppermute(east, "lon", eastward)
    from_east = lax.ppermute(west, "lon", [(b, a) for a, b in eastward])
    part = call(middle, inner, [inner32] + work_space((144, 144)), 2_000_000_000, x, gain, w_qkv, w_out)
    north, south = call(pack_lat, (edge, edge), [pltpu.VMEM((72, WIDTH), F32)], 1_000_000, x, from_west, from_east)
    from_south = lax.ppermute(north, "lat", northward)
    from_north = lax.ppermute(south, "lat", [(b, a) for a, b in northward])
    part = call(
        sides, inner, [inner32, edge32, edge32] + work_space((80,) * 4), 2_000_000_000,
        x, from_west, from_east, part, gain, w_qkv, w_out,
    )
    poles32 = pltpu.VMEM((2 * SHIFT, LON, WIDTH), F32)
    mixed = call(
        poles, jax.ShapeDtypeStruct((LAT, LON, WIDTH), BF),
        [poles32] + [edge32] * 4 + work_space((80, 48, 48) * 2), 2_000_000_000,
        pole_mask, x, from_west, from_east, from_south, from_north, part, gain, w_qkv, w_out, smem=1,
    )
    return jnp.transpose(mixed, (1, 0, 2))


def solution(mesh):
    in_specs = (P("lon", "lat", None), P(), P(), P(), P())
    out_specs = P("lon", "lat", None)
    return jax.shard_map(shards, mesh=mesh, in_specs=in_specs, out_specs=out_specs, check_vma=False)
```

time: 162 us -> 40.2 us (0.25)
  the two profiles are of different devices: /device:TPU:2 before, /device:TPU:8 now
where the time goes in v1:
time: 40.2 us; the launch traced here: 39.9 us
  starting transfers between devices  20.7 us (51%)
  Pallas kernels  12.4 us (31%)
  waiting for transfers between devices  5.51 us (14%)
  local copies, waits for them, and re-layouts  1.18 us (3%)
    ppermute x1, starting transfers between devices, shards(): from_east = lax.ppermute(west, 'lon', [(b, a) for a, b in eastward])  12.6 us
    pallas_call x5, Pallas kernels, call(): pl.pallas_call(body, out_shape=out_shape, in_specs=specs, out_specs=jax.t...  12.4 us
    ppermute x1, starting transfers between devices, shards(): from_south = lax.ppermute(north, 'lat', northward)  4.18 us
    ppermute x1, waiting for transfers between devices, shards(): from_north = lax.ppermute(south, 'lat', [(b, a) for a, b in northward])  2.08 us
    ppermute x1, starting transfers between devices, shards(): from_west = lax.ppermute(east, 'lon', eastward)  2.05 us
    ppermute x1, starting transfers between devices, shards(): from_north = lax.ppermute(south, 'lat', [(b, a) for a, b in northward])  1.92 us
    ppermute x1, waiting for transfers between devices, shards(): from_east = lax.ppermute(west, 'lon', [(b, a) for a, b in eastward])  1.76 us
    ppermute x1, waiting for transfers between devices, shards(): from_west = lax.ppermute(east, 'lon', eastward)  1.67 us
  transfers between devices with their start and end apart: 4, of which 3 were waited for; matrix products, arithmetic and copies ran while one was open for 0% of the time, Pallas kernels for 12%

profile of v1, /device:TPU:8, one launch (start us, length us, event | category | flops | bytes accessed | tf_op | source)
XLA Modules:
  0.0 39.9 jit_solution(13870676092525916696)
XLA Ops:
  0.0 0.0 copy-start
  0.0 1.2 %copy-done = bf16[24,36,512]{2,0,1:T(8,128)(2,1)S(1)} copy-done((bf16[24,36,512]{2,0,1:T(8,128)(2,1)S(1)}, bf16[24,36,512]{2,0,1:T(8,128)(2,1)}, u32[]{:S(2)}) %copy-start) | copy-done | bytes 884760
  1.2 0.0 copy-start.1
  1.2 0.0 copy-start.2
  1.2 0.0 copy-start.4
  1.2 0.1 shard_map.55
  1.3 2.1 %collective-permute-start = (bf16[216,512]{1,0:T(8,128)(2,1)S(1)}, bf16[216,512]{1,0:T(8,128)(2,1)S(1)}, u32[]{:S(2)}, u32[]{:S(2)}) collective-permute-start(bf16[216,512]{1,0:T(8,128)(2,1)S(1)} %get-tuple-element.9), channel_id=1, source_target_pairs={{0,8},{8,16},{16,24},{24,32},{32,40},{40,48},{48,56},{56,64},{64,7... | collective-permute-start | bytes 663560 | tf_op jit(solution)/shard_map/ppermute | solution.py:236
  3.4 12.6 %collective-permute-start.1 = (bf16[216,512]{1,0:T(8,128)(2,1)S(1)}, bf16[216,512]{1,0:T(8,128)(2,1)S(1)}, u32[]{:S(2)}, u32[]{:S(2)}) collective-permute-start(bf16[216,512]{1,0:T(8,128)(2,1)S(1)} %get-tuple-element.10), channel_id=1, source_target_pairs={{8,0},{16,8},{24,16},{32,24},{40,32},{48,40},{56,48},{64,56},{72,6... | collective-permute-start | bytes 663560 | tf_op jit(solution)/shard_map/ppermute | solution.py:237
  16.0 1.7 %collective-permute-done.from_west = bf16[216,512]{1,0:T(8,128)(2,1)S(1)} collective-permute-done((bf16[216,512]{1,0:T(8,128)(2,1)S(1)}, bf16[216,512]{1,0:T(8,128)(2,1)S(1)}, u32[]{:S(2)}, u32[]{:S(2)}) %collective-permute-start) | collective-permute-done | bytes 221216 | tf_op jit(solution)/shard_map/ppermute | solution.py:236
  17.6 1.8 %collective-permute-done.1.from_east = bf16[216,512]{1,0:T(8,128)(2,1)S(1)} collective-permute-done((bf16[216,512]{1,0:T(8,128)(2,1)S(1)}, bf16[216,512]{1,0:T(8,128)(2,1)S(1)}, u32[]{:S(2)}, u32[]{:S(2)}) %collective-permute-start.1) | collective-permute-done | bytes 221216 | tf_op jit(solution)/shard_map/ppermute | solution.py:237
  19.4 4.2 %collective-permute-start.2 = (bf16[216,512]{1,0:T(8,128)(2,1)S(1)}, bf16[216,512]{1,0:T(8,128)(2,1)S(1)}, u32[]{:S(2)}, u32[]{:S(2)}) collective-permute-start(bf16[216,512]{1,0:T(8,128)(2,1)S(1)} %get-tuple-element.11), channel_id=1, source_target_pairs={{0,1},{1,2},{2,3},{3,4},{4,5},{5,6},{6,7},{8,9},{9,10},{10,11},{11... | collective-permute-start | bytes 663560 | tf_op jit(solution)/shard_map/ppermute | solution.py:240
  23.6 1.9 %collective-permute-start.3 = (bf16[216,512]{1,0:T(8,128)(2,1)S(1)}, bf16[216,512]{1,0:T(8,128)(2,1)S(1)}, u32[]{:S(2)}, u32[]{:S(2)}) collective-permute-start(bf16[216,512]{1,0:T(8,128)(2,1)S(1)} %get-tuple-element.12), channel_id=1, source_target_pairs={{1,0},{2,1},{3,2},{4,3},{5,4},{6,5},{7,6},{9,8},{10,9},{11,10},{12... | collective-permute-start | bytes 663560 | tf_op jit(solution)/shard_map/ppermute | solution.py:241
  25.6 0.0 copy-done.1
  25.6 0.0 copy-done.2
  25.6 0.0 copy-done.4
  25.6 2.0 %shard_map.57.done = bf16[24,24,512]{2,1,0:T(8,128)(2,1)S(1)} custom-call(bf16[36,24,512]{2,1,0:T(8,128)(2,1)S(1)} %bitcast.5, f32[1,512]{1,0:T(1,128)S(1)} %bitcast.8, bf16[512,1536]{1,0:T(8,128)(2,1)S(1)} %copy-done.1, bf16[512,512]{1,0:T(8,128)(2,1)S(1)} %copy-done.2), custom_call_target="tpu_custom_call" | custom-call | flops 2000000000 | bytes 4000000 | tf_op jit(solution)/shard_map/pallas_call | solution.py:214
  27.6 0.0 copy-start.3
  27.6 2.6 %shard_map.58.done = bf16[24,24,512]{2,1,0:T(8,128)(2,1)S(1)} custom-call(bf16[36,24,512]{2,1,0:T(8,128)(2,1)S(1)} %bitcast.6, bf16[216,512]{1,0:T(8,128)(2,1)S(1)} %collective-permute-done.from_west, bf16[216,512]{1,0:T(8,128)(2,1)S(1)} %collective-permute-done.1.from_east, bf16[24,24,512]{2,1,0:T(8,128)(2,1)S(1)} %shard_map.57.done, f32[1,512]{1,0:T(1,128)S(1)} %bitcast.9, ...), custom_call_target="tpu_custom_call" | custom-call | flops 2000000000 | bytes 4000000 | tf_op jit(solution)/shard_map/pallas_call | solution.py:214
  30.3 0.0 collective-permute-done.2.from_south
  30.3 2.1 %collective-permute-done.3.from_north = bf16[216,512]{1,0:T(8,128)(2,1)S(1)} collective-permute-done((bf16[216,512]{1,0:T(8,128)(2,1)S(1)}, bf16[216,512]{1,0:T(8,128)(2,1)S(1)}, u32[]{:S(2)}, u32[]{:S(2)}) %collective-permute-start.3) | collective-permute-done | bytes 221216 | tf_op jit(solution)/shard_map/ppermute | solution.py:241
  32.4 0.0 copy-done.3
  32.4 7.6 %shard_map.59 = bf16[36,24,512]{2,1,0:T(8,128)(2,1)} custom-call(s32[288]{0:T(512)S(1)} %copy-done.3, bf16[36,24,512]{2,1,0:T(8,128)(2,1)S(1)} %bitcast.7, bf16[216,512]{1,0:T(8,128)(2,1)S(1)} %collective-permute-done.from_west, bf16[216,512]{1,0:T(8,128)(2,1)S(1)} %collective-permute-done.1.from_east, ...), custom_call_target="tpu_custom_call" | custom-call | flops 2000000000 | bytes 4000000 | tf_op jit(solution)/shard_map/pallas_call | solution.py:214
  (1 shorter events, 0.0 us)
Async XLA Ops:
  0.0 1.2 %copy-start = (bf16[24,36,512]{2,0,1:T(8,128)(2,1)S(1)}, bf16[24,36,512]{2,0,1:T(8,128)(2,1)}, u32[]{:S(2)}) copy-start(bf16[24,36,512]{2,0,1:T(8,128)(2,1)} %param.5) | copy-start | bytes 2654212
  1.2 24.4 %copy-start.1 = (bf16[512,1536]{1,0:T(8,128)(2,1)S(1)}, bf16[512,1536]{1,0:T(8,128)(2,1)}, u32[]{:S(2)}) copy-start(bf16[512,1536]{1,0:T(8,128)(2,1)} %w_qkv.5) | copy-start | bytes 4718596
  1.2 24.4 %copy-start.2 = (bf16[512,512]{1,0:T(8,128)(2,1)S(1)}, bf16[512,512]{1,0:T(8,128)(2,1)}, u32[]{:S(2)}) copy-start(bf16[512,512]{1,0:T(8,128)(2,1)} %w_out.5) | copy-start | bytes 1572868
  1.2 24.4 %copy-start.4 = (f32[512]{0:T(512)S(1)}, f32[512]{0:T(512)}, u32[]{:S(2)}) copy-start(f32[512]{0:T(512)} %param.6) | copy-start | bytes 6148
  1.3 16.3 %collective-permute-start = (bf16[216,512]{1,0:T(8,128)(2,1)S(1)}, bf16[216,512]{1,0:T(8,128)(2,1)S(1)}, u32[]{:S(2)}, u32[]{:S(2)}) collective-permute-start(bf16[216,512]{1,0:T(8,128)(2,1)S(1)} %get-tuple-element.9), channel_id=1, source_target_pairs={{0,8},{8,16},{16,24},{24,32},{32,40},{40,48},{48,56},{56,64},{64,7... | collective-permute-start | bytes 663560 | tf_op jit(solution)/shard_map/ppermute | solution.py:236
  3.4 16.0 %collective-permute-start.1 = (bf16[216,512]{1,0:T(8,128)(2,1)S(1)}, bf16[216,512]{1,0:T(8,128)(2,1)S(1)}, u32[]{:S(2)}, u32[]{:S(2)}) collective-permute-start(bf16[216,512]{1,0:T(8,128)(2,1)S(1)} %get-tuple-element.10), channel_id=1, source_target_pairs={{8,0},{16,8},{24,16},{32,24},{40,32},{48,40},{56,48},{64,56},{72,6... | collective-permute-start | bytes 663560 | tf_op jit(solution)/shard_map/ppermute | solution.py:237
  19.4 10.8 %collective-permute-start.2 = (bf16[216,512]{1,0:T(8,128)(2,1)S(1)}, bf16[216,512]{1,0:T(8,128)(2,1)S(1)}, u32[]{:S(2)}, u32[]{:S(2)}) collective-permute-start(bf16[216,512]{1,0:T(8,128)(2,1)S(1)} %get-tuple-element.11), channel_id=1, source_target_pairs={{0,1},{1,2},{2,3},{3,4},{4,5},{5,6},{6,7},{8,9},{9,10},{10,11},{11... | collective-permute-start | bytes 663560 | tf_op jit(solution)/shard_map/ppermute | solution.py:240
  23.6 8.7 %collective-permute-start.3 = (bf16[216,512]{1,0:T(8,128)(2,1)S(1)}, bf16[216,512]{1,0:T(8,128)(2,1)S(1)}, u32[]{:S(2)}, u32[]{:S(2)}) collective-permute-start(bf16[216,512]{1,0:T(8,128)(2,1)S(1)} %get-tuple-element.12), channel_id=1, source_target_pairs={{1,0},{2,1},{3,2},{4,3},{5,4},{6,5},{7,6},{9,8},{10,9},{11,10},{12... | collective-permute-start | bytes 663560 | tf_op jit(solution)/shard_map/ppermute | solution.py:241
  27.6 4.7 %copy-start.3 = (s32[288]{0:T(512)S(1)}, s32[288]{0:T(512)}, u32[]{:S(2)}) copy-start(s32[288]{0:T(512)} %mask.1) | copy-start | bytes 3460

commit v2 on v1

v2 whole, which is shorter than its diff:
```python
import functools

import jax
import jax.numpy as jnp
from jax import lax
from jax.experimental import pallas as pl
from jax.experimental.pallas import tpu as pltpu
from jax.sharding import PartitionSpec as P

WIDTH = 512
HEADS = 8
WINDOW = 12
SHIFT = 6
KEYS = WINDOW * WINDOW
EPS = 1e-05
NLAT = 288
LON = 24
LAT = 36
EDGE = LAT * SHIFT
HALF = 80
BF = jnp.bfloat16
F32 = jnp.float32


def normalise(window_tokens, gain, normed, block):
    for start in range(0, normed.shape[0], block):
        values = window_tokens[start : start + block, :].astype(F32)
        average = jnp.sum(values, axis=-1, keepdims=True) * (1.0 / WIDTH)
        centred = values - average
        variance = jnp.sum(centred * centred, axis=-1, keepdims=True) * (1.0 / WIDTH)
        normed[start : start + block, :] = (centred * lax.rsqrt(variance + EPS) * gain).astype(BF)


def project_pairs(normed, w_qkv, pairs):
    for col in range(0, 2 * WIDTH, 256):
        part = jnp.dot(normed[...], w_qkv[:, WIDTH + col : WIDTH + col + 256], preferred_element_type=F32)
        pairs[:, col : col + 256] = part.astype(BF)


def project_queries(rows, w_qkv, queries):
    for col in range(0, WIDTH, 256):
        part = jnp.dot(rows[...], w_qkv[:, col : col + 256], preferred_element_type=F32)
        queries[:, col : col + 256] = (part.astype(BF).astype(F32) * (WIDTH // HEADS) ** (-0.5)).astype(BF)


def window_context(queries, q_base, count, key_parts, context, bias):
    lane = lax.broadcasted_iota(jnp.int32, (1, 128), 1)
    low32 = lane < 64
    keep_low = low32.astype(F32).astype(BF)
    keep_high = (lane >= 64).astype(F32).astype(BF)
    ones = jnp.ones((sum(part[2] for part in key_parts), 128), BF)

    def rows_of(col):
        found = [ref[base : base + rows, col : col + 128] for ref, base, rows in key_parts]
        return found[0] if len(found) == 1 else jnp.concatenate(found, axis=0)

    for pair in range(HEADS // 2):
        cols = slice(128 * pair, 128 * pair + 128)
        both = queries[q_base : q_base + count, cols]
        stacked = jnp.concatenate([both * keep_low, both * keep_high], axis=0)
        key_part, value_part = rows_of(128 * pair), rows_of(WIDTH + 128 * pair)
        scores = lax.dot_general(stacked, key_part, (((1,), (1,)), ((), ())), preferred_element_type=F32)
        if bias is not None:
            scores = scores + bias
        row_max = jnp.max(scores, axis=-1, keepdims=True)
        exp_scores = jnp.exp(scores - row_max).astype(BF)
        widened = jnp.concatenate([value_part, ones], axis=1)
        summed = jnp.dot(exp_scores, widened, preferred_element_type=F32)
        first, second = summed[:count], summed[count:]
        top = jnp.where(low32, first[:, :128], second[:, :128])
        under = jnp.where(low32, first[:, 128:], second[:, 128:])
        context[q_base : q_base + count, cols] = (top / under).astype(BF)


def finish(context, w_out, residual, stride, count, mixed):
    for col in range(0, WIDTH, 256):
        part = jnp.dot(context[...], w_out[:, col : col + 256], preferred_element_type=F32)
        for index in range(mixed.shape[0] // count):
            here = slice(count * index, count * index + count)
            own = residual[stride * index : stride * index + count, col : col + 256].astype(F32)
            mixed[here, col : col + 256] = part[here] + own


def attend(window_tokens, gain_ref, w_qkv, w_out, count, normed, q_rows, pairs, queries, context, mixed):
    windows = normed.shape[0] // KEYS
    normalise(window_tokens, gain_ref[...], normed, KEYS)
    for index in range(windows):
        q_rows[count * index : count * index + count, :] = normed[KEYS * index : KEYS * index + count, :]
    project_pairs(normed, w_qkv, pairs)
    project_queries(q_rows, w_qkv, queries)
    for index in range(windows):
        window_context(queries, count * index, count, [(pairs, KEYS * index, KEYS)], context, None)
    finish(context, w_out, window_tokens, KEYS, count, mixed)


def pack_lon(x, east, west, east32, west32):
    for lat in range(LAT):
        row = x[lat].astype(F32)
        west32[SHIFT * lat : SHIFT * lat + SHIFT, :] = row[0:SHIFT]
        east32[SHIFT * lat : SHIFT * lat + SHIFT, :] = row[LON - SHIFT : LON]
    west[...] = west32[...].astype(BF)
    east[...] = east32[...].astype(BF)


def pack_lat(x, from_west, from_east, north, south, work):
    own = SHIFT * LON
    for target, lat, halo in ((south, 0, 0), (north, LAT - SHIFT, EDGE - 36)):
        target[0:own, :] = x[lat : lat + SHIFT].reshape(own, WIDTH)
        work[0:36, :] = from_west[...].astype(F32)[halo : halo + 36]
        work[36:72, :] = from_east[...].astype(F32)[halo : halo + 36]
        target[own : own + 72, :] = work[...].astype(BF)


def middle(x, gain, w_qkv, w_out, out, x32, stack, normed, q_rows, pairs, queries, context, mixed):
    x32[...] = x[SHIFT : LAT - SHIFT].astype(F32)
    for lat in range(24):
        stack[12 * lat : 12 * lat + 12, :] = x32[lat, 6:18, :]
    attend(stack, gain, w_qkv, w_out, KEYS, normed, q_rows, pairs, queries, context, mixed)
    for lat in range(24):
        x32[lat, 6:18, :] = mixed[12 * lat : 12 * lat + 12, :]
    out[...] = x32[...].astype(BF)


def sides(x, from_west, from_east, done, gain, w_qkv, w_out, out, x32, w32, e32, stack, normed, q_rows, pairs, queries, context, mixed):
    x32[...] = x[SHIFT : LAT - SHIFT].astype(F32)
    w32[...] = from_west[...].astype(F32)
    e32[...] = from_east[...].astype(F32)
    for index in range(4):
        band, east = index // 2, index % 2
        lon = 18 if east else 0
        base = KEYS * index
        for step in range(12):
            stack[base + 6 * step : base + 6 * step + 6, :] = x32[12 * band + step, lon : lon + 6, :]
        halo = e32 if east else w32
        stack[base + 72 : base + 144, :] = halo[36 + 72 * band : 108 + 72 * band, :]
    attend(stack, gain, w_qkv, w_out, HALF, normed, q_rows, pairs, queries, context, mixed)
    x32[...] = done[...].astype(F32)
    for index in range(4):
        band, east = index // 2, index % 2
        lon = 18 if east else 0
        for step in range(12):
            x32[12 * band + step, lon : lon + 6, :] = mixed[HALF * index + 6 * step : HALF * index + 6 * step + 6, :]
    out[...] = x32[...].astype(BF)


def prepare(x, from_west, from_east, gain, w_qkv, raw, queries, pairs, x32, w32, e32, stack, normed):
    x32[0:SHIFT] = x[0:SHIFT].astype(F32)
    x32[SHIFT : 2 * SHIFT] = x[LAT - SHIFT : LAT].astype(F32)
    w32[...] = from_west[...].astype(F32)
    e32[...] = from_east[...].astype(F32)
    for north in range(2):
        base = 3 * HALF * north
        for step in range(SHIFT):
            at = SHIFT * north + step
            stack[base + 12 * step : base + 12 * step + 12, :] = x32[at, 6:18, :]
            stack[base + 80 + 6 * step : base + 86 + 6 * step, :] = x32[at, 0:6, :]
            stack[base + 160 + 6 * step : base + 166 + 6 * step, :] = x32[at, 18:24, :]
        halo = EDGE - 36 if north else 0
        stack[base + 116 : base + 152, :] = w32[halo : halo + 36, :]
        stack[base + 196 : base + 232, :] = e32[halo : halo + 36, :]
        for window in range(3):
            stack[base + 80 * window + 72 : base + 80 * window + 80, :] = jnp.zeros((8, WIDTH), F32)
    raw[...] = stack[...].astype(BF)
    normalise(raw, gain[...], normed, HALF)
    project_pairs(normed, w_qkv, pairs)
    project_queries(normed, w_qkv, queries)


def pole_bias(mask, band, north):
    key = lax.broadcasted_iota(jnp.int32, (1, 2 * HALF), 1)
    in_halo = key >= HALF
    inner = jnp.where(in_halo, key - HALF, key)
    row_wide = inner // 12
    row_corner = jnp.where(inner >= 36, inner - 36, inner) // 6
    real = inner < 72
    bias_wide = jnp.full((1, 2 * HALF), -1e30, F32)
    bias_corner = bias_wide
    lat_at = band * LAT + (LAT - SHIFT if north else 0)
    halo_at = band * LAT + (LAT if north else -SHIFT)
    for step in range(SHIFT):
        there = halo_at + step
        exists = jnp.logical_and(there >= 0, there < NLAT)
        halo_ok = jnp.logical_and(exists, mask[jnp.clip(there, 0, NLAT - 1)] == 1)
        own_bias = jnp.where(mask[lat_at + step] == 1, 0.0, -1e30)
        halo_bias = jnp.where(halo_ok, 0.0, -1e30)
        step_bias = jnp.where(in_halo, halo_bias, own_bias)
        bias_wide = jnp.where(jnp.logical_and(real, row_wide == step), step_bias, bias_wide)
        bias_corner = jnp.where(jnp.logical_and(real, row_corner == step), step_bias, bias_corner)
    return bias_wide, bias_corner


def poles(
    mask, raw, queries, own_pairs, from_south, from_north, done, gain, w_qkv, w_out, out,
    s32, n32, stack, normed, pairs, context, mixed, x32, rows, sem,
):
    inner_copy = pltpu.make_async_copy(done, out.at[SHIFT : LAT - SHIFT], sem.at[0])
    inner_copy.start()
    s32[...] = from_south[...].astype(F32)
    n32[...] = from_north[...].astype(F32)
    band = lax.axis_index("lat")
    biases = []
    for north in range(2):
        halo = n32 if north else s32
        base = 3 * HALF * north
        for step in range(SHIFT):
            at = LON * step
            stack[base + 12 * step : base + 12 * step + 12, :] = halo[at + 6 : at + 18, :]
            stack[base + 80 + 6 * step : base + 86 + 6 * step, :] = halo[at : at + 6, :]
            stack[base + 160 + 6 * step : base + 166 + 6 * step, :] = halo[at + 18 : at + 24, :]
        stack[base + 116 : base + 152, :] = halo[144:180, :]
        stack[base + 196 : base + 232, :] = halo[180:216, :]
        for window in range(3):
            stack[base + 80 * window + 72 : base + 80 * window + 80, :] = jnp.zeros((8, WIDTH), F32)
        wide, corner = pole_bias(mask, band, north)
        biases += [wide, corner, corner]
    normalise(stack, gain[...], normed, HALF)
    project_pairs(normed, w_qkv, pairs)
    for index in range(6):
        at = HALF * index
        window_context(queries, at, HALF, [(own_pairs, at, HALF), (pairs, at, HALF)], context, biases[index])
    finish(context, w_out, raw, HALF, HALF, mixed)
    for north in range(2):
        base = 3 * HALF * north
        for step in range(SHIFT):
            at = SHIFT * north + step
            x32[at, 6:18, :] = mixed[base + 12 * step : base + 12 * step + 12, :]
            x32[at, 0:6, :] = mixed[base + 80 + 6 * step : base + 86 + 6 * step, :]
            x32[at, 18:24, :] = mixed[base + 160 + 6 * step : base + 166 + 6 * step, :]
    rows[...] = x32[...].astype(BF)
    south_copy = pltpu.make_async_copy(rows.at[0:SHIFT], out.at[0:SHIFT], sem.at[1])
    north_copy = pltpu.make_async_copy(rows.at[SHIFT : 2 * SHIFT], out.at[LAT - SHIFT : LAT], sem.at[2])
    south_copy.start()
    north_copy.start()
    inner_copy.wait()
    south_copy.wait()
    north_copy.wait()


def vmem(rows, columns=WIDTH, dtype=BF):
    return pltpu.VMEM((rows, columns), dtype)


def work_space(windows, count):
    total, asked = KEYS * windows, count * windows
    return [
        vmem(total, dtype=F32), vmem(total), vmem(asked), vmem(total, 2 * WIDTH),
        vmem(asked), vmem(asked), vmem(asked, dtype=F32),
    ]


def call(body, out_shape, scratch, flops, *operands, smem=0, in_hbm=False):
    whole = pl.BlockSpec(memory_space=pltpu.VMEM)
    out_spec = pl.BlockSpec(memory_space=pl.ANY) if in_hbm else whole
    specs = [pl.BlockSpec(memory_space=pltpu.SMEM)] * smem + [whole] * (len(operands) - smem)
    return pl.pallas_call(
        body,
        out_shape=out_shape,
        in_specs=specs,
        out_specs=jax.tree.map(lambda _: out_spec, out_shape),
        scratch_shapes=scratch,
        compiler_params=pltpu.CompilerParams(vmem_limit_bytes=40 * 2**20),
        cost_estimate=pl.CostEstimate(flops=flops, bytes_accessed=4_000_000, transcendentals=0),
    )(*operands)


def shards(tokens, norm_gain, w_qkv, w_out, pole_mask):
    x = jnp.transpose(tokens, (1, 0, 2))
    gain = norm_gain.reshape(1, WIDTH)
    lons, lats = lax.axis_size("lon"), lax.axis_size("lat")
    eastward = [(i, (i + 1) % lons) for i in range(lons)]
    northward = [(i, i + 1) for i in range(lats - 1)]
    edge = jax.ShapeDtypeStruct((EDGE, WIDTH), BF)
    inner = jax.ShapeDtypeStruct((LAT - 2 * SHIFT, LON, WIDTH), BF)
    edge32 = vmem(EDGE, dtype=F32)
    inner32 = pltpu.VMEM((LAT - 2 * SHIFT, LON, WIDTH), F32)
    poles32 = pltpu.VMEM((2 * SHIFT, LON, WIDTH), F32)
    east, west = call(pack_lon, (edge, edge), [edge32, edge32], 8_000_000_000, x)
    from_west = lax.ppermute(east, "lon", eastward)
    from_east = lax.ppermute(west, "lon", [(b, a) for a, b in eastward])
    part = call(middle, inner, [inner32] + work_space(2, KEYS), 2_000_000_000, x, gain, w_qkv, w_out)
    part, from_west, from_east = lax.optimization_barrier((part, from_west, from_east))
    north, south = call(pack_lat, (edge, edge), [vmem(72, dtype=F32)], 1_000_000, x, from_west, from_east)
    from_south = lax.ppermute(north, "lat", northward)
    from_north = lax.ppermute(south, "lat", [(b, a) for a, b in northward])
    part = call(
        sides, inner, [inner32, edge32, edge32] + work_space(4, HALF), 2_000_000_000,
        x, from_west, from_east, part, gain, w_qkv, w_out,
    )
    rows = 6 * HALF
    raw, queries, pairs = call(
        prepare, tuple(jax.ShapeDtypeStruct((rows, n), BF) for n in (WIDTH, WIDTH, 2 * WIDTH)),
        [poles32, edge32, edge32, vmem(rows, dtype=F32), vmem(rows)], 2_000_000_000,
        x, from_west, from_east, gain, w_qkv,
    )
    mixed = call(
        poles, jax.ShapeDtypeStruct((LAT, LON, WIDTH), BF),
        [
            edge32, edge32, vmem(rows, dtype=F32), vmem(rows), vmem(rows, 2 * WIDTH), vmem(rows), vmem(rows, dtype=F32),
            poles32, pltpu.VMEM((2 * SHIFT, LON, WIDTH), BF), pltpu.SemaphoreType.DMA((3,)),
        ], 2_000_000_000,
        pole_mask, raw, queries, pairs, from_south, from_north, part, gain, w_qkv, w_out, smem=1, in_hbm=True,
    )
    return jnp.transpose(mixed, (1, 0, 2))


def solution(mesh):
    in_specs = (P("lon", "lat", None), P(), P(), P(), P())
    out_specs = P("lon", "lat", None)
    return jax.shard_map(shards, mesh=mesh, in_specs=in_specs, out_specs=out_specs, check_vma=False)
```

time: 40.2 us -> 36.6 us (0.910)
  Pallas kernels: 12.4 us -> 10.2 us
  waiting for transfers between devices: 5.51 us -> 4.19 us
    pallas_call x5 -> x6, Pallas kernels: 12.4 us -> 10.2 us  [call(): pl.pallas_call(body, out_shape=out_shape, in_specs=specs, out_specs=jax.t...]
    ppermute x1, waiting for transfers between devices: 1.67 us -> 0.01 us  [shards(): from_west = lax.ppermute(east, 'lon', eastward)]
    ppermute x1, waiting for transfers between devices: 2.08 us -> 2.83 us  [shards(): from_north = lax.ppermute(south, 'lat', [(b, a) for a, b in northward])]
    ppermute x1, waiting for transfers between devices: 1.76 us -> 1.35 us  [shards(): from_east = lax.ppermute(west, 'lon', [(b, a) for a, b in eastward])]
  transfers between devices with their start and end apart: 4 -> 4, of which waited for: 3 -> 2; matrix products, arithmetic and copies ran while one was open for 0% -> 0% of each run, Pallas kernels for 12% -> 16%
where the time goes in v2:
time: 36.6 us; the launch traced here: 36.4 us
  starting transfers between devices  20.7 us (57%)
  Pallas kernels  10.2 us (28%)
  waiting for transfers between devices  4.19 us (11%)
  local copies, waits for them, and re-layouts  1.18 us (3%)
    ppermute x1, starting transfers between devices, shards(): from_east = lax.ppermute(west, 'lon', [(b, a) for a, b in eastward])  12.6 us
    pallas_call x6, Pallas kernels, call(): pl.pallas_call(body, out_shape=out_shape, in_specs=specs, out_specs=jax.t...  10.2 us
    ppermute x1, starting transfers between devices, shards(): from_south = lax.ppermute(north, 'lat', northward)  4.18 us
    ppermute x1, waiting for transfers between devices, shards(): from_north = lax.ppermute(south, 'lat', [(b, a) for a, b in northward])  2.83 us
    ppermute x1, starting transfers between devices, shards(): from_west = lax.ppermute(east, 'lon', eastward)  2.05 us
    ppermute x1, starting transfers between devices, shards(): from_north = lax.ppermute(south, 'lat', [(b, a) for a, b in northward])  1.92 us
    ppermute x1, waiting for transfers between devices, shards(): from_east = lax.ppermute(west, 'lon', [(b, a) for a, b in eastward])  1.35 us
    unnamed x10, local copies, waits for them, and re-layouts  1.18 us
  transfers between devices with their start and end apart: 4, of which 2 were waited for; matrix products, arithmetic and copies ran while one was open for 0% of the time, Pallas kernels for 16%

profile of v2, /device:TPU:8, one launch (start us, length us, event | category | flops | bytes accessed | tf_op | source)
XLA Modules:
  0.0 36.4 jit_solution(8083027775365372339)
XLA Ops:
  0.0 0.0 copy-start
  0.0 1.2 %copy-done = bf16[24,36,512]{2,0,1:T(8,128)(2,1)S(1)} copy-done((bf16[24,36,512]{2,0,1:T(8,128)(2,1)S(1)}, bf16[24,36,512]{2,0,1:T(8,128)(2,1)}, u32[]{:S(2)}) %copy-start) | copy-done | bytes 884760
  1.2 0.0 copy-start.1
  1.2 0.0 copy-start.2
  1.2 0.0 copy-start.4
  1.2 0.1 shard_map.56
  1.3 2.1 %collective-permute-start = (bf16[216,512]{1,0:T(8,128)(2,1)S(1)}, bf16[216,512]{1,0:T(8,128)(2,1)S(1)}, u32[]{:S(2)}, u32[]{:S(2)}) collective-permute-start(bf16[216,512]{1,0:T(8,128)(2,1)S(1)} %get-tuple-element.15), channel_id=1, source_target_pairs={{0,8},{8,16},{16,24},{24,32},{32,40},{40,48},{48,56},{56,64},{64,7... | collective-permute-start | bytes 663560 | tf_op jit(solution)/shard_map/ppermute | solution.py:278
  3.4 12.6 %collective-permute-start.1 = (bf16[216,512]{1,0:T(8,128)(2,1)S(1)}, bf16[216,512]{1,0:T(8,128)(2,1)S(1)}, u32[]{:S(2)}, u32[]{:S(2)}) collective-permute-start(bf16[216,512]{1,0:T(8,128)(2,1)S(1)} %get-tuple-element.16), channel_id=1, source_target_pairs={{8,0},{16,8},{24,16},{32,24},{40,32},{48,40},{56,48},{64,56},{72,6... | collective-permute-start | bytes 663560 | tf_op jit(solution)/shard_map/ppermute | solution.py:279
  16.0 0.0 copy-done.1
  16.0 0.0 copy-done.2
  16.0 0.0 copy-done.4
  16.0 2.0 %shard_map.55.done = bf16[24,24,512]{2,1,0:T(8,128)(2,1)S(1)} custom-call(bf16[36,24,512]{2,1,0:T(8,128)(2,1)S(1)} %bitcast.4, f32[1,512]{1,0:T(1,128)S(1)} %bitcast.8, bf16[512,1536]{1,0:T(8,128)(2,1)S(1)} %copy-done.1, bf16[512,512]{1,0:T(8,128)(2,1)S(1)} %copy-done.2), custom_call_target="tpu_custom_call" | custom-call | flops 2000000000 | bytes 4000000 | tf_op jit(solution)/shard_map/pallas_call | solution.py:255
  18.0 0.0 collective-permute-done.from_west
  18.0 1.4 %collective-permute-done.1.from_east = bf16[216,512]{1,0:T(8,128)(2,1)S(1)} collective-permute-done((bf16[216,512]{1,0:T(8,128)(2,1)S(1)}, bf16[216,512]{1,0:T(8,128)(2,1)S(1)}, u32[]{:S(2)}, u32[]{:S(2)}) %collective-permute-start.1) | collective-permute-done | bytes 221216 | tf_op jit(solution)/shard_map/ppermute | solution.py:279
  19.4 4.2 %collective-permute-start.2 = (bf16[216,512]{1,0:T(8,128)(2,1)S(1)}, bf16[216,512]{1,0:T(8,128)(2,1)S(1)}, u32[]{:S(2)}, u32[]{:S(2)}) collective-permute-start(bf16[216,512]{1,0:T(8,128)(2,1)S(1)} %get-tuple-element.22), channel_id=1, source_target_pairs={{0,1},{1,2},{2,3},{3,4},{4,5},{5,6},{6,7},{8,9},{9,10},{10,11},{11... | collective-permute-start | bytes 663560 | tf_op jit(solution)/shard_map/ppermute | solution.py:283
  23.6 1.9 %collective-permute-start.3 = (bf16[216,512]{1,0:T(8,128)(2,1)S(1)}, bf16[216,512]{1,0:T(8,128)(2,1)S(1)}, u32[]{:S(2)}, u32[]{:S(2)}) collective-permute-start(bf16[216,512]{1,0:T(8,128)(2,1)S(1)} %get-tuple-element.23), channel_id=1, source_target_pairs={{1,0},{2,1},{3,2},{4,3},{5,4},{6,5},{7,6},{9,8},{10,9},{11,10},{12... | collective-permute-start | bytes 663560 | tf_op jit(solution)/shard_map/ppermute | solution.py:284
  25.6 1.3 %shard_map.57 = (bf16[480,512]{1,0:T(8,128)(2,1)S(1)}, bf16[480,512]{1,0:T(8,128)(2,1)S(1)}, bf16[480,1024]{1,0:T(8,128)(2,1)S(1)}) custom-call(bf16[36,24,512]{2,1,0:T(8,128)(2,1)S(1)} %bitcast.6, bf16[216,512]{1,0:T(8,128)(2,1)S(1)} %collective-permute-done.from_west, bf16[216,512]{1,0:T(8,128)(2,1)S(1)} %collective-permute-done.1.from_east, ...), custom_call_target="tpu_custom_call" | custom-call | flops 2000000000 | bytes 4000000 | tf_op jit(solution)/shard_map/pallas_call | solution.py:255
  26.9 0.0 copy-start.3
  26.9 2.6 %shard_map.59.done = bf16[24,24,512]{2,1,0:T(8,128)(2,1)S(1)} custom-call(bf16[36,24,512]{2,1,0:T(8,128)(2,1)S(1)} %bitcast.7, bf16[216,512]{1,0:T(8,128)(2,1)S(1)} %collective-permute-done.from_west, bf16[216,512]{1,0:T(8,128)(2,1)S(1)} %collective-permute-done.1.from_east, bf16[24,24,512]{2,1,0:T(8,128)(2,1)S(1)} %shard_map.55.done, ...), custom_call_target="tpu_custom_call" | custom-call | flops 2000000000 | bytes 4000000 | tf_op jit(solution)/shard_map/pallas_call | solution.py:255
  29.5 0.0 collective-permute-done.2.from_south
  29.5 2.8 %collective-permute-done.3.from_north = bf16[216,512]{1,0:T(8,128)(2,1)S(1)} collective-permute-done((bf16[216,512]{1,0:T(8,128)(2,1)S(1)}, bf16[216,512]{1,0:T(8,128)(2,1)S(1)}, u32[]{:S(2)}, u32[]{:S(2)}) %collective-permute-start.3) | collective-permute-done | bytes 221216 | tf_op jit(solution)/shard_map/ppermute | solution.py:284
  32.4 0.0 copy-done.3
  32.4 4.0 %shard_map.60 = bf16[36,24,512]{2,1,0:T(8,128)(2,1)} custom-call(s32[288]{0:T(512)S(1)} %copy-done.3, bf16[480,512]{1,0:T(8,128)(2,1)S(1)} %get-tuple-element.19.raw, bf16[480,512]{1,0:T(8,128)(2,1)S(1)} %get-tuple-element.20.queries, bf16[480,1024]{1,0:T(8,128)(2,1)S(1)} %get-tuple-element.21.own_pairs, ...), custom_call_target="tpu_custom_call" | custom-call | flops 2000000000 | bytes 4000000 | tf_op jit(solution)/shard_map/pallas_call | solution.py:255
  (1 shorter events, 0.0 us)
Async XLA Ops:
  0.0 1.2 %copy-start = (bf16[24,36,512]{2,0,1:T(8,128)(2,1)S(1)}, bf16[24,36,512]{2,0,1:T(8,128)(2,1)}, u32[]{:S(2)}) copy-start(bf16[24,36,512]{2,0,1:T(8,128)(2,1)} %param.5) | copy-start | bytes 2654212
  1.2 14.8 %copy-start.1 = (bf16[512,1536]{1,0:T(8,128)(2,1)S(1)}, bf16[512,1536]{1,0:T(8,128)(2,1)}, u32[]{:S(2)}) copy-start(bf16[512,1536]{1,0:T(8,128)(2,1)} %w_qkv.7) | copy-start | bytes 4718596
  1.2 14.8 %copy-start.2 = (bf16[512,512]{1,0:T(8,128)(2,1)S(1)}, bf16[512,512]{1,0:T(8,128)(2,1)}, u32[]{:S(2)}) copy-start(bf16[512,512]{1,0:T(8,128)(2,1)} %w_out.5) | copy-start | bytes 1572868
  1.2 14.8 %copy-start.4 = (f32[512]{0:T(512)S(1)}, f32[512]{0:T(512)}, u32[]{:S(2)}) copy-start(f32[512]{0:T(512)} %param.6) | copy-start | bytes 6148
  1.3 16.7 %collective-permute-start = (bf16[216,512]{1,0:T(8,128)(2,1)S(1)}, bf16[216,512]{1,0:T(8,128)(2,1)S(1)}, u32[]{:S(2)}, u32[]{:S(2)}) collective-permute-start(bf16[216,512]{1,0:T(8,128)(2,1)S(1)} %get-tuple-element.15), channel_id=1, source_target_pairs={{0,8},{8,16},{16,24},{24,32},{32,40},{40,48},{48,56},{56,64},{64,7... | collective-permute-start | bytes 663560 | tf_op jit(solution)/shard_map/ppermute | solution.py:278
  3.4 16.0 %collective-permute-start.1 = (bf16[216,512]{1,0:T(8,128)(2,1)S(1)}, bf16[216,512]{1,0:T(8,128)(2,1)S(1)}, u32[]{:S(2)}, u32[]{:S(2)}) collective-permute-start(bf16[216,512]{1,0:T(8,128)(2,1)S(1)} %get-tuple-element.16), channel_id=1, source_target_pairs={{8,0},{16,8},{24,16},{32,24},{40,32},{48,40},{56,48},{64,56},{72,6... | collective-permute-start | bytes 663560 | tf_op jit(solution)/shard_map/ppermute | solution.py:279
  19.4 10.1 %collective-permute-start.2 = (bf16[216,512]{1,0:T(8,128)(2,1)S(1)}, bf16[216,512]{1,0:T(8,128)(2,1)S(1)}, u32[]{:S(2)}, u32[]{:S(2)}) collective-permute-start(bf16[216,512]{1,0:T(8,128)(2,1)S(1)} %get-tuple-element.22), channel_id=1, source_target_pairs={{0,1},{1,2},{2,3},{3,4},{4,5},{5,6},{6,7},{8,9},{9,10},{10,11},{11... | collective-permute-start | bytes 663560 | tf_op jit(solution)/shard_map/ppermute | solution.py:283
  23.6 8.7 %collective-permute-start.3 = (bf16[216,512]{1,0:T(8,128)(2,1)S(1)}, bf16[216,512]{1,0:T(8,128)(2,1)S(1)}, u32[]{:S(2)}, u32[]{:S(2)}) collective-permute-start(bf16[216,512]{1,0:T(8,128)(2,1)S(1)} %get-tuple-element.23), channel_id=1, source_target_pairs={{1,0},{2,1},{3,2},{4,3},{5,4},{6,5},{7,6},{9,8},{10,9},{11,10},{12... | collective-permute-start | bytes 663560 | tf_op jit(solution)/shard_map/ppermute | solution.py:284
  26.9 5.5 %copy-start.3 = (s32[288]{0:T(512)S(1)}, s32[288]{0:T(512)}, u32[]{:S(2)}) copy-start(s32[288]{0:T(512)} %mask.1) | copy-start | bytes 3460

commit v3 on v2

--- a/solution.py
+++ b/solution.py
@@ -43,7 +43,7 @@
         queries[:, col : col + 256] = (part.astype(BF).astype(F32) * (WIDTH // HEADS) ** (-0.5)).astype(BF)
 
 
-def window_context(queries, q_base, count, key_parts, context, bias):
+def window_context(queries, q_base, c_base, count, key_parts, context, bias):
     lane = lax.broadcasted_iota(jnp.int32, (1, 128), 1)
     low32 = lane < 64
     keep_low = low32.astype(F32).astype(BF)
@@ -69,15 +69,15 @@
         first, second = summed[:count], summed[count:]
         top = jnp.where(low32, first[:, :128], second[:, :128])
         under = jnp.where(low32, first[:, 128:], second[:, 128:])
-        context[q_base : q_base + count, cols] = (top / under).astype(BF)
-
-
-def finish(context, w_out, residual, stride, count, mixed):
+        context[c_base : c_base + count, cols] = (top / under).astype(BF)
+
+
+def finish(context, w_out, residual, base, stride, count, mixed):
     for col in range(0, WIDTH, 256):
         part = jnp.dot(context[...], w_out[:, col : col + 256], preferred_element_type=F32)
         for index in range(mixed.shape[0] // count):
             here = slice(count * index, count * index + count)
-            own = residual[stride * index : stride * index + count, col : col + 256].astype(F32)
+            own = residual[base + stride * index : base + stride * index + count, col : col + 256].astype(F32)
             mixed[here, col : col + 256] = part[here] + own
 
 
@@ -89,8 +89,8 @@
     project_pairs(normed, w_qkv, pairs)
     project_queries(q_rows, w_qkv, queries)
     for index in range(windows):
-        window_context(queries, count * index, count, [(pairs, KEYS * index, KEYS)], context, None)
-    finish(context, w_out, window_tokens, KEYS, count, mixed)
+        window_context(queries, count * index, count * index, count, [(pairs, KEYS * index, KEYS)], context, None)
+    finish(context, w_out, window_tokens, 0, KEYS, count, mixed)
 
 
 def pack_lon(x, east, west, east32, west32):
@@ -121,26 +121,29 @@
     out[...] = x32[...].astype(BF)
 
 
-def sides(x, from_west, from_east, done, gain, w_qkv, w_out, out, x32, w32, e32, stack, normed, q_rows, pairs, queries, context, mixed):
+def side_windows(east, x, halo, done, gain, w_qkv, w_out, out, x32, halo32, stack, normed, q_rows, pairs, queries, context, mixed):
+    lon = LON - SHIFT if east else 0
     x32[...] = x[SHIFT : LAT - SHIFT].astype(F32)
-    w32[...] = from_west[...].astype(F32)
-    e32[...] = from_east[...].astype(F32)
-    for index in range(4):
-        band, east = index // 2, index % 2
-        lon = 18 if east else 0
-        base = KEYS * index
+    halo32[...] = halo[...].astype(F32)
+    for band in range(2):
+        base = KEYS * band
         for step in range(12):
             stack[base + 6 * step : base + 6 * step + 6, :] = x32[12 * band + step, lon : lon + 6, :]
-        halo = e32 if east else w32
-        stack[base + 72 : base + 144, :] = halo[36 + 72 * band : 108 + 72 * band, :]
+        stack[base + 72 : base + 144, :] = halo32[36 + 72 * band : 108 + 72 * band, :]
     attend(stack, gain, w_qkv, w_out, HALF, normed, q_rows, pairs, queries, context, mixed)
     x32[...] = done[...].astype(F32)
-    for index in range(4):
-        band, east = index // 2, index % 2
-        lon = 18 if east else 0
+    for band in range(2):
         for step in range(12):
-            x32[12 * band + step, lon : lon + 6, :] = mixed[HALF * index + 6 * step : HALF * index + 6 * step + 6, :]
+            x32[12 * band + step, lon : lon + 6, :] = mixed[HALF * band + 6 * step : HALF * band + 6 * step + 6, :]
     out[...] = x32[...].astype(BF)
+
+
+def west_side(*refs):
+    side_windows(False, *refs)
+
+
+def east_side(*refs):
+    side_windows(True, *refs)
 
 
 def prepare(x, from_west, from_east, gain, w_qkv, raw, queries, pairs, x32, w32, e32, stack, normed):
@@ -189,51 +192,53 @@
     return bias_wide, bias_corner
 
 
-def poles(
-    mask, raw, queries, own_pairs, from_south, from_north, done, gain, w_qkv, w_out, out,
-    s32, n32, stack, normed, pairs, context, mixed, x32, rows, sem,
+def pole_windows(
+    north, mask, raw, queries, own_pairs, arrived, gain, w_qkv, w_out, result,
+    halo, stack, normed, pairs, context, mixed, x32,
 ):
-    inner_copy = pltpu.make_async_copy(done, out.at[SHIFT : LAT - SHIFT], sem.at[0])
-    inner_copy.start()
-    s32[...] = from_south[...].astype(F32)
-    n32[...] = from_north[...].astype(F32)
-    band = lax.axis_index("lat")
-    biases = []
-    for north in range(2):
-        halo = n32 if north else s32
-        base = 3 * HALF * north
-        for step in range(SHIFT):
-            at = LON * step
-            stack[base + 12 * step : base + 12 * step + 12, :] = halo[at + 6 : at + 18, :]
-            stack[base + 80 + 6 * step : base + 86 + 6 * step, :] = halo[at : at + 6, :]
-            stack[base + 160 + 6 * step : base + 166 + 6 * step, :] = halo[at + 18 : at + 24, :]
-        stack[base + 116 : base + 152, :] = halo[144:180, :]
-        stack[base + 196 : base + 232, :] = halo[180:216, :]
-        for window in range(3):
-            stack[base + 80 * window + 72 : base + 80 * window + 80, :] = jnp.zeros((8, WIDTH), F32)
-        wide, corner = pole_bias(mask, band, north)
-        biases += [wide, corner, corner]
+    halo[...] = arrived[...].astype(F32)
+    for step in range(SHIFT):
+        at = LON * step
+        stack[12 * step : 12 * step + 12, :] = halo[at + 6 : at + 18, :]
+        stack[80 + 6 * step : 86 + 6 * step, :] = halo[at : at + 6, :]
+        stack[160 + 6 * step : 166 + 6 * step, :] = halo[at + 18 : at + 24, :]
+    stack[116:152, :] = halo[144:180, :]
+    stack[196:232, :] = halo[180:216, :]
+    for window in range(3):
+        stack[80 * window + 72 : 80 * window + 80, :] = jnp.zeros((8, WIDTH), F32)
+    wide, corner = pole_bias(mask, lax.axis_index("lat"), north)
     normalise(stack, gain[...], normed, HALF)
     project_pairs(normed, w_qkv, pairs)
-    for index in range(6):
+    base = 3 * HALF * north
+    for index, bias in enumerate((wide, corner, corner)):
         at = HALF * index
-        window_context(queries, at, HALF, [(own_pairs, at, HALF), (pairs, at, HALF)], context, biases[index])
-    finish(context, w_out, raw, HALF, HALF, mixed)
-    for north in range(2):
-        base = 3 * HALF * north
-        for step in range(SHIFT):
-            at = SHIFT * north + step
-            x32[at, 6:18, :] = mixed[base + 12 * step : base + 12 * step + 12, :]
-            x32[at, 0:6, :] = mixed[base + 80 + 6 * step : base + 86 + 6 * step, :]
-            x32[at, 18:24, :] = mixed[base + 160 + 6 * step : base + 166 + 6 * step, :]
-    rows[...] = x32[...].astype(BF)
-    south_copy = pltpu.make_async_copy(rows.at[0:SHIFT], out.at[0:SHIFT], sem.at[1])
-    north_copy = pltpu.make_async_copy(rows.at[SHIFT : 2 * SHIFT], out.at[LAT - SHIFT : LAT], sem.at[2])
-    south_copy.start()
-    north_copy.start()
-    inner_copy.wait()
-    south_copy.wait()
-    north_copy.wait()
+        parts = [(own_pairs, base + at, HALF), (pairs, at, HALF)]
+        window_context(queries, base + at, at, HALF, parts, context, bias)
+    finish(context, w_out, raw, base, HALF, HALF, mixed)
+    for step in range(SHIFT):
+        x32[step, 6:18, :] = mixed[12 * step : 12 * step + 12, :]
+        x32[step, 0:6, :] = mixed[80 + 6 * step : 86 + 6 * step, :]
+        x32[step, 18:24, :] = mixed[160 + 6 * step : 166 + 6 * step, :]
+    result[...] = x32[...].astype(BF)
+
+
+def south_pole(*refs):
+    pole_windows(0, *refs)
+
+
+def north_pole(mask, raw, queries, own_pairs, arrived, inner, south, gain, w_qkv, w_out, out, *scratch):
+    *work, rows, sem = scratch
+    copies = [
+        pltpu.make_async_copy(inner, out.at[SHIFT : LAT - SHIFT], sem.at[0]),
+        pltpu.make_async_copy(south, out.at[0:SHIFT], sem.at[1]),
+        pltpu.make_async_copy(rows, out.at[LAT - SHIFT : LAT], sem.at[2]),
+    ]
+    copies[0].start()
+    copies[1].start()
+    pole_windows(1, mask, raw, queries, own_pairs, arrived, gain, w_qkv, w_out, rows, *work)
+    copies[2].start()
+    for copy in copies:
+        copy.wait()
 
 
 def vmem(rows, columns=WIDTH, dtype=BF):
@@ -259,7 +264,7 @@
         out_specs=jax.tree.map(lambda _: out_spec, out_shape),
         scratch_shapes=scratch,
         compiler_params=pltpu.CompilerParams(vmem_limit_bytes=40 * 2**20),
-        cost_estimate=pl.CostEstimate(flops=flops, bytes_accessed=4_000_000, transcendentals=0),
+        cost_estimate=pl.CostEstimate(flops=flops, bytes_accessed=flops // 1000, transcendentals=0),
     )(*operands)
 
 
@@ -278,27 +283,33 @@
     from_west = lax.ppermute(east, "lon", eastward)
     from_east = lax.ppermute(west, "lon", [(b, a) for a, b in eastward])
     part = call(middle, inner, [inner32] + work_space(2, KEYS), 2_000_000_000, x, gain, w_qkv, w_out)
+    part, from_west = lax.optimization_barrier((part, from_west))
+    side_work = [inner32, edge32] + work_space(2, HALF)
+    part = call(west_side, inner, side_work, 1_000_000, x, from_west, part, gain, w_qkv, w_out)
     part, from_west, from_east = lax.optimization_barrier((part, from_west, from_east))
     north, south = call(pack_lat, (edge, edge), [vmem(72, dtype=F32)], 1_000_000, x, from_west, from_east)
     from_south = lax.ppermute(north, "lat", northward)
     from_north = lax.ppermute(south, "lat", [(b, a) for a, b in northward])
-    part = call(
-        sides, inner, [inner32, edge32, edge32] + work_space(4, HALF), 2_000_000_000,
-        x, from_west, from_east, part, gain, w_qkv, w_out,
-    )
+    part = call(east_side, inner, side_work, 1_000_000, x, from_east, part, gain, w_qkv, w_out)
     rows = 6 * HALF
     raw, queries, pairs = call(
         prepare, tuple(jax.ShapeDtypeStruct((rows, n), BF) for n in (WIDTH, WIDTH, 2 * WIDTH)),
-        [poles32, edge32, edge32, vmem(rows, dtype=F32), vmem(rows)], 2_000_000_000,
+        [poles32, edge32, edge32, vmem(rows, dtype=F32), vmem(rows)], 1_000_000,
         x, from_west, from_east, gain, w_qkv,
     )
+    half = rows // 2
+    work = [edge32, vmem(half, dtype=F32), vmem(half), vmem(half, 2 * WIDTH), vmem(half), vmem(half, dtype=F32)]
+    work.append(pltpu.VMEM((SHIFT, LON, WIDTH), F32))
+    part, from_south = lax.optimization_barrier((part, from_south))
+    low = call(
+        south_pole, jax.ShapeDtypeStruct((SHIFT, LON, WIDTH), BF), work, 1_000_000,
+        pole_mask, raw, queries, pairs, from_south, gain, w_qkv, w_out, smem=1,
+    )
+    low, from_north = lax.optimization_barrier((low, from_north))
     mixed = call(
-        poles, jax.ShapeDtypeStruct((LAT, LON, WIDTH), BF),
-        [
-            edge32, edge32, vmem(rows, dtype=F32), vmem(rows), vmem(rows, 2 * WIDTH), vmem(rows), vmem(rows, dtype=F32),
-            poles32, pltpu.VMEM((2 * SHIFT, LON, WIDTH), BF), pltpu.SemaphoreType.DMA((3,)),
-        ], 2_000_000_000,
-        pole_mask, raw, queries, pairs, from_south, from_north, part, gain, w_qkv, w_out, smem=1, in_hbm=True,
+        north_pole, jax.ShapeDtypeStruct((LAT, LON, WIDTH), BF),
+        work + [pltpu.VMEM((SHIFT, LON, WIDTH), BF), pltpu.SemaphoreType.DMA((3,))], 2_000_000_000,
+        pole_mask, raw, queries, pairs, from_north, part, low, gain, w_qkv, w_out, smem=1, in_hbm=True,
     )
     return jnp.transpose(mixed, (1, 0, 2))
 

time: 36.6 us -> 35.7 us (0.975)
  the two profiles are of different devices: /device:TPU:8 before, /device:TPU:2 now
where the time goes in v3:
time: 35.7 us; the launch traced here: 35.3 us
  starting transfers between devices  22.3 us (62%)
  Pallas kernels  11.6 us (32%)
  local copies, waits for them, and re-layouts  1.18 us (3%)
    ppermute x1, starting transfers between devices, shards(): from_east = lax.ppermute(west, 'lon', [(b, a) for a, b in eastward])  13.5 us
    pallas_call x8, Pallas kernels, call(): pl.pallas_call(body, out_shape=out_shape, in_specs=specs, out_specs=jax.t...  11.6 us
    ppermute x1, starting transfers between devices, shards(): from_north = lax.ppermute(south, 'lat', [(b, a) for a, b in northward])  4.15 us
    ppermute x1, starting transfers between devices, shards(): from_south = lax.ppermute(north, 'lat', northward)  2.59 us
    ppermute x1, starting transfers between devices, shards(): from_west = lax.ppermute(east, 'lon', eastward)  2.05 us
    unnamed x10, local copies, waits for them, and re-layouts  1.18 us
  transfers between devices with their start and end apart: 4, of which 0 were waited for; matrix products, arithmetic and copies ran while one was open for 0% of the time, Pallas kernels for 25%

profile of v3, /device:TPU:2, one launch (start us, length us, event | category | flops | bytes accessed | tf_op | source)
XLA Modules:
  0.0 35.3 jit_solution(10129660178063836900)
XLA Ops:
  0.0 0.0 copy-start.1
  0.0 1.2 %copy-done.1 = bf16[24,36,512]{2,0,1:T(8,128)(2,1)S(1)} copy-done((bf16[24,36,512]{2,0,1:T(8,128)(2,1)S(1)}, bf16[24,36,512]{2,0,1:T(8,128)(2,1)}, u32[]{:S(2)}) %copy-start.1) | copy-done | bytes 884760
  1.2 0.0 copy-start
  1.2 0.0 copy-start.2
  1.2 0.0 copy-start.3
  1.2 0.1 shard_map.56
  1.3 2.1 %collective-permute-start = (bf16[216,512]{1,0:T(8,128)(2,1)S(1)}, bf16[216,512]{1,0:T(8,128)(2,1)S(1)}, u32[]{:S(2)}, u32[]{:S(2)}) collective-permute-start(bf16[216,512]{1,0:T(8,128)(2,1)S(1)} %get-tuple-element.21), channel_id=1, source_target_pairs={{0,8},{8,16},{16,24},{24,32},{32,40},{40,48},{48,56},{56,64},{64,7... | collective-permute-start | bytes 663560 | tf_op jit(solution)/shard_map/ppermute | solution.py:283
  3.4 13.5 %collective-permute-start.1 = (bf16[216,512]{1,0:T(8,128)(2,1)S(1)}, bf16[216,512]{1,0:T(8,128)(2,1)S(1)}, u32[]{:S(2)}, u32[]{:S(2)}) collective-permute-start(bf16[216,512]{1,0:T(8,128)(2,1)S(1)} %get-tuple-element.24), channel_id=1, source_target_pairs={{8,0},{16,8},{24,16},{32,24},{40,32},{48,40},{56,48},{64,56},{72,6... | collective-permute-start | bytes 663560 | tf_op jit(solution)/shard_map/ppermute | solution.py:284
  16.9 0.0 copy-done
  16.9 0.0 copy-done.2
  16.9 0.0 copy-done.3
  16.9 2.0 %shard_map.55.refs_2_ = bf16[24,24,512]{2,1,0:T(8,128)(2,1)S(1)} custom-call(bf16[36,24,512]{2,1,0:T(8,128)(2,1)S(1)} %bitcast.4, f32[1,512]{1,0:T(1,128)S(1)} %bitcast.9, bf16[512,1536]{1,0:T(8,128)(2,1)S(1)} %copy-done, bf16[512,512]{1,0:T(8,128)(2,1)S(1)} %copy-done.2), custom_call_target="tpu_custom_call" | custom-call | flops 2000000000 | bytes 2000000 | tf_op jit(solution)/shard_map/pallas_call | solution.py:260
  18.9 0.0 collective-permute-done.refs_1_.from_west
  18.9 1.6 %shard_map.57.refs_2_ = bf16[24,24,512]{2,1,0:T(8,128)(2,1)S(1)} custom-call(bf16[36,24,512]{2,1,0:T(8,128)(2,1)S(1)} %bitcast.5, bf16[216,512]{1,0:T(8,128)(2,1)S(1)} %collective-permute-done.refs_1_.from_west, bf16[24,24,512]{2,1,0:T(8,128)(2,1)S(1)} %shard_map.55.refs_2_, f32[1,512]{1,0:T(1,128)S(1)} %bitcast.10, bf16[512,1536]{1,0:T(8,128)(2,1)S(1)} %copy-done, ...), custom_call_target="tpu_custom_call" | custom-call | flops 1000000 | bytes 1000 | tf_op jit(solution)/shard_map/pallas_call | solution.py:260
  20.6 0.0 collective-permute-done.1.from_east.refs_1_
  20.6 2.6 %collective-permute-start.2 = (bf16[216,512]{1,0:T(8,128)(2,1)S(1)}, bf16[216,512]{1,0:T(8,128)(2,1)S(1)}, u32[]{:S(2)}, u32[]{:S(2)}) collective-permute-start(bf16[216,512]{1,0:T(8,128)(2,1)S(1)} %get-tuple-element.31), channel_id=1, source_target_pairs={{0,1},{1,2},{2,3},{3,4},{4,5},{5,6},{6,7},{8,9},{9,10},{10,11},{11... | collective-permute-start | bytes 663560 | tf_op jit(solution)/shard_map/ppermute | solution.py:291
  23.2 4.2 %collective-permute-start.3 = (bf16[216,512]{1,0:T(8,128)(2,1)S(1)}, bf16[216,512]{1,0:T(8,128)(2,1)S(1)}, u32[]{:S(2)}, u32[]{:S(2)}) collective-permute-start(bf16[216,512]{1,0:T(8,128)(2,1)S(1)} %get-tuple-element.33), channel_id=1, source_target_pairs={{1,0},{2,1},{3,2},{4,3},{5,4},{6,5},{7,6},{9,8},{10,9},{11,10},{12... | collective-permute-start | bytes 663560 | tf_op jit(solution)/shard_map/ppermute | solution.py:292
  27.4 1.3 %shard_map.58 = (bf16[480,512]{1,0:T(8,128)(2,1)S(1)}, bf16[480,512]{1,0:T(8,128)(2,1)S(1)}, bf16[480,1024]{1,0:T(8,128)(2,1)S(1)}) custom-call(bf16[36,24,512]{2,1,0:T(8,128)(2,1)S(1)} %bitcast.7, bf16[216,512]{1,0:T(8,128)(2,1)S(1)} %collective-permute-done.refs_1_.from_west, bf16[216,512]{1,0:T(8,128)(2,1)S(1)} %collective-permute-done.1.from_east.refs_1_, ...), custom_call_target="tpu_custom_call" | custom-call | flops 1000000 | bytes 1000 | tf_op jit(solution)/shard_map/pallas_call | solution.py:260
  28.7 0.0 copy-start.4
  28.7 1.6 %shard_map.59.inner = bf16[24,24,512]{2,1,0:T(8,128)(2,1)S(1)} custom-call(bf16[36,24,512]{2,1,0:T(8,128)(2,1)S(1)} %bitcast.8, bf16[216,512]{1,0:T(8,128)(2,1)S(1)} %collective-permute-done.1.from_east.refs_1_, bf16[24,24,512]{2,1,0:T(8,128)(2,1)S(1)} %shard_map.57.refs_2_, f32[1,512]{1,0:T(1,128)S(1)} %bitcast.12, bf16[512,1536]{1,0:T(8,128)(2,1)S(1)} %copy-done, ...), custom_call_target="tpu_custom_call" | custom-call | flops 1000000 | bytes 1000 | tf_op jit(solution)/shard_map/pallas_call | solution.py:260
  30.3 0.0 collective-permute-done.2.refs_4_
  30.3 0.0 copy-done.4
  30.3 2.1 %shard_map.61.south = bf16[6,24,512]{2,1,0:T(8,128)(2,1)S(1)} custom-call(s32[288]{0:T(512)S(1)} %copy-done.4, bf16[480,512]{1,0:T(8,128)(2,1)S(1)} %get-tuple-element.27.refs_1_.raw, bf16[480,512]{1,0:T(8,128)(2,1)S(1)} %get-tuple-element.28.refs_2_.queries, bf16[480,1024]{1,0:T(8,128)(2,1)S(1)} %get-tuple-element.29.refs_3_.own_pairs, ...), custom_call_target="tpu_custom_call" | custom-call | flops 1000000 | bytes 1000 | tf_op jit(solution)/shard_map/pallas_call | solution.py:260
  32.4 0.0 collective-permute-done.3.arrived
  32.4 2.8 %shard_map.62 = bf16[36,24,512]{2,1,0:T(8,128)(2,1)} custom-call(s32[288]{0:T(512)S(1)} %copy-done.4, bf16[480,512]{1,0:T(8,128)(2,1)S(1)} %get-tuple-element.27.refs_1_.raw, bf16[480,512]{1,0:T(8,128)(2,1)S(1)} %get-tuple-element.28.refs_2_.queries, bf16[480,1024]{1,0:T(8,128)(2,1)S(1)} %get-tuple-element.29.refs_3_.own_pairs, ...), custom_call_target="tpu_custom_call" | custom-call | flops 2000000000 | bytes 2000000 | tf_op jit(solution)/shard_map/pallas_call | solution.py:260
  (1 shorter events, 0.0 us)
Async XLA Ops:
  0.0 1.2 %copy-start.1 = (bf16[24,36,512]{2,0,1:T(8,128)(2,1)S(1)}, bf16[24,36,512]{2,0,1:T(8,128)(2,1)}, u32[]{:S(2)}) copy-start(bf16[24,36,512]{2,0,1:T(8,128)(2,1)} %param.5) | copy-start | bytes 2654212
  1.2 15.7 %copy-start = (bf16[512,1536]{1,0:T(8,128)(2,1)S(1)}, bf16[512,1536]{1,0:T(8,128)(2,1)}, u32[]{:S(2)}) copy-start(bf16[512,1536]{1,0:T(8,128)(2,1)} %w_qkv.5) | copy-start | bytes 4718596
  1.2 15.7 %copy-start.2 = (bf16[512,512]{1,0:T(8,128)(2,1)S(1)}, bf16[512,512]{1,0:T(8,128)(2,1)}, u32[]{:S(2)}) copy-start(bf16[512,512]{1,0:T(8,128)(2,1)} %w_out.3) | copy-start | bytes 1572868
  1.2 15.7 %copy-start.3 = (f32[512]{0:T(512)S(1)}, f32[512]{0:T(512)}, u32[]{:S(2)}) copy-start(f32[512]{0:T(512)} %param.6) | copy-start | bytes 6148
  1.3 17.6 %collective-permute-start = (bf16[216,512]{1,0:T(8,128)(2,1)S(1)}, bf16[216,512]{1,0:T(8,128)(2,1)S(1)}, u32[]{:S(2)}, u32[]{:S(2)}) collective-permute-start(bf16[216,512]{1,0:T(8,128)(2,1)S(1)} %get-tuple-element.21), channel_id=1, source_target_pairs={{0,8},{8,16},{16,24},{24,32},{32,40},{40,48},{48,56},{56,64},{64,7... | collective-permute-start | bytes 663560 | tf_op jit(solution)/shard_map/ppermute | solution.py:283
  3.4 17.2 %collective-permute-start.1 = (bf16[216,512]{1,0:T(8,128)(2,1)S(1)}, bf16[216,512]{1,0:T(8,128)(2,1)S(1)}, u32[]{:S(2)}, u32[]{:S(2)}) collective-permute-start(bf16[216,512]{1,0:T(8,128)(2,1)S(1)} %get-tuple-element.24), channel_id=1, source_target_pairs={{8,0},{16,8},{24,16},{32,24},{40,32},{48,40},{56,48},{64,56},{72,6... | collective-permute-start | bytes 663560 | tf_op jit(solution)/shard_map/ppermute | solution.py:284
  20.6 9.7 %collective-permute-start.2 = (bf16[216,512]{1,0:T(8,128)(2,1)S(1)}, bf16[216,512]{1,0:T(8,128)(2,1)S(1)}, u32[]{:S(2)}, u32[]{:S(2)}) collective-permute-start(bf16[216,512]{1,0:T(8,128)(2,1)S(1)} %get-tuple-element.31), channel_id=1, source_target_pairs={{0,1},{1,2},{2,3},{3,4},{4,5},{5,6},{6,7},{8,9},{9,10},{10,11},{11... | collective-permute-start | bytes 663560 | tf_op jit(solution)/shard_map/ppermute | solution.py:291
  23.2 9.2 %collective-permute-start.3 = (bf16[216,512]{1,0:T(8,128)(2,1)S(1)}, bf16[216,512]{1,0:T(8,128)(2,1)S(1)}, u32[]{:S(2)}, u32[]{:S(2)}) collective-permute-start(bf16[216,512]{1,0:T(8,128)(2,1)S(1)} %get-tuple-element.33), channel_id=1, source_target_pairs={{1,0},{2,1},{3,2},{4,3},{5,4},{6,5},{7,6},{9,8},{10,9},{11,10},{12... | collective-permute-start | bytes 663560 | tf_op jit(solution)/shard_map/ppermute | solution.py:292
  28.7 1.7 %copy-start.4 = (s32[288]{0:T(512)S(1)}, s32[288]{0:T(512)}, u32[]{:S(2)}) copy-start(s32[288]{0:T(512)} %mask.1) | copy-start | bytes 3460

commit v4 on v3

--- a/solution.py
+++ b/solution.py
@@ -51,12 +51,12 @@
     ones = jnp.ones((sum(part[2] for part in key_parts), 128), BF)
 
     def rows_of(col):
-        found = [ref[base : base + rows, col : col + 128] for ref, base, rows in key_parts]
+        found = [ref[pl.ds(base, rows), col : col + 128] for ref, base, rows in key_parts]
         return found[0] if len(found) == 1 else jnp.concatenate(found, axis=0)
 
     for pair in range(HEADS // 2):
         cols = slice(128 * pair, 128 * pair + 128)
-        both = queries[q_base : q_base + count, cols]
+        both = queries[pl.ds(q_base, count), cols]
         stacked = jnp.concatenate([both * keep_low, both * keep_high], axis=0)
         key_part, value_part = rows_of(128 * pair), rows_of(WIDTH + 128 * pair)
         scores = lax.dot_general(stacked, key_part, (((1,), (1,)), ((), ())), preferred_element_type=F32)
@@ -77,7 +77,7 @@
         part = jnp.dot(context[...], w_out[:, col : col + 256], preferred_element_type=F32)
         for index in range(mixed.shape[0] // count):
             here = slice(count * index, count * index + count)
-            own = residual[base + stride * index : base + stride * index + count, col : col + 256].astype(F32)
+            own = residual[pl.ds(base + stride * index, count), col : col + 256].astype(F32)
             mixed[here, col : col + 256] = part[here] + own
 
 
@@ -102,13 +102,28 @@
     east[...] = east32[...].astype(BF)
 
 
-def pack_lat(x, from_west, from_east, north, south, work):
+def first_is_north():
+    return 1 - lax.axis_index("lat") % 2
+
+
+def pack_lat(x, from_west, from_east, first, second, work):
     own = SHIFT * LON
-    for target, lat, halo in ((south, 0, 0), (north, LAT - SHIFT, EDGE - 36)):
+
+    def put(target, lat, halo):
         target[0:own, :] = x[lat : lat + SHIFT].reshape(own, WIDTH)
         work[0:36, :] = from_west[...].astype(F32)[halo : halo + 36]
         work[36:72, :] = from_east[...].astype(F32)[halo : halo + 36]
         target[own : own + 72, :] = work[...].astype(BF)
+
+    @pl.when(first_is_north() == 1)
+    def _():
+        put(first, LAT - SHIFT, EDGE - 36)
+        put(second, 0, 0)
+
+    @pl.when(first_is_north() == 0)
+    def _():
+        put(first, 0, 0)
+        put(second, LAT - SHIFT, EDGE - 36)
 
 
 def middle(x, gain, w_qkv, w_out, out, x32, stack, normed, q_rows, pairs, queries, context, mixed):
@@ -178,8 +193,8 @@
     real = inner < 72
     bias_wide = jnp.full((1, 2 * HALF), -1e30, F32)
     bias_corner = bias_wide
-    lat_at = band * LAT + (LAT - SHIFT if north else 0)
-    halo_at = band * LAT + (LAT if north else -SHIFT)
+    lat_at = band * LAT + (LAT - SHIFT) * north
+    halo_at = band * LAT + (LAT + SHIFT) * north - SHIFT
     for step in range(SHIFT):
         there = halo_at + step
         exists = jnp.logical_and(there >= 0, there < NLAT)
@@ -209,7 +224,7 @@
     wide, corner = pole_bias(mask, lax.axis_index("lat"), north)
     normalise(stack, gain[...], normed, HALF)
     project_pairs(normed, w_qkv, pairs)
-    base = 3 * HALF * north
+    base = pl.multiple_of(3 * HALF * north, 3 * HALF)
     for index, bias in enumerate((wide, corner, corner)):
         at = HALF * index
         parts = [(own_pairs, base + at, HALF), (pairs, at, HALF)]
@@ -222,20 +237,22 @@
     result[...] = x32[...].astype(BF)
 
 
-def south_pole(*refs):
-    pole_windows(0, *refs)
-
-
-def north_pole(mask, raw, queries, own_pairs, arrived, inner, south, gain, w_qkv, w_out, out, *scratch):
+def first_pole(*refs):
+    pole_windows(first_is_north(), *refs)
+
+
+def second_pole(mask, raw, queries, own_pairs, arrived, inner, early, gain, w_qkv, w_out, out, *scratch):
     *work, rows, sem = scratch
+    north = 1 - first_is_north()
+    far = LAT - SHIFT
     copies = [
         pltpu.make_async_copy(inner, out.at[SHIFT : LAT - SHIFT], sem.at[0]),
-        pltpu.make_async_copy(south, out.at[0:SHIFT], sem.at[1]),
-        pltpu.make_async_copy(rows, out.at[LAT - SHIFT : LAT], sem.at[2]),
+        pltpu.make_async_copy(early, out.at[pl.ds(far - far * north, SHIFT)], sem.at[1]),
+        pltpu.make_async_copy(rows, out.at[pl.ds(far * north, SHIFT)], sem.at[2]),
     ]
     copies[0].start()
     copies[1].start()
-    pole_windows(1, mask, raw, queries, own_pairs, arrived, gain, w_qkv, w_out, rows, *work)
+    pole_windows(north, mask, raw, queries, own_pairs, arrived, gain, w_qkv, w_out, rows, *work)
     copies[2].start()
     for copy in copies:
         copy.wait()
@@ -287,9 +304,9 @@
     side_work = [inner32, edge32] + work_space(2, HALF)
     part = call(west_side, inner, side_work, 1_000_000, x, from_west, part, gain, w_qkv, w_out)
     part, from_west, from_east = lax.optimization_barrier((part, from_west, from_east))
-    north, south = call(pack_lat, (edge, edge), [vmem(72, dtype=F32)], 1_000_000, x, from_west, from_east)
-    from_south = lax.ppermute(north, "lat", northward)
-    from_north = lax.ppermute(south, "lat", [(b, a) for a, b in northward])
+    first, second = call(pack_lat, (edge, edge), [vmem(72, dtype=F32)], 1_000_000, x, from_west, from_east)
+    met_first = lax.ppermute(first, "lat", [pair for a, b in northward[0::2] for pair in ((a, b), (b, a))])
+    met_second = lax.ppermute(second, "lat", [pair for a, b in northward[1::2] for pair in ((a, b), (b, a))])
     part = call(east_side, inner, side_work, 1_000_000, x, from_east, part, gain, w_qkv, w_out)
     rows = 6 * HALF
     raw, queries, pairs = call(
@@ -300,16 +317,16 @@
     half = rows // 2
     work = [edge32, vmem(half, dtype=F32), vmem(half), vmem(half, 2 * WIDTH), vmem(half), vmem(half, dtype=F32)]
     work.append(pltpu.VMEM((SHIFT, LON, WIDTH), F32))
-    part, from_south = lax.optimization_barrier((part, from_south))
-    low = call(
-        south_pole, jax.ShapeDtypeStruct((SHIFT, LON, WIDTH), BF), work, 1_000_000,
-        pole_mask, raw, queries, pairs, from_south, gain, w_qkv, w_out, smem=1,
+    part, met_first = lax.optimization_barrier((part, met_first))
+    early = call(
+        first_pole, jax.ShapeDtypeStruct((SHIFT, LON, WIDTH), BF), work, 1_000_000,
+        pole_mask, raw, queries, pairs, met_first, gain, w_qkv, w_out, smem=1,
     )
-    low, from_north = lax.optimization_barrier((low, from_north))
+    early, met_second = lax.optimization_barrier((early, met_second))
     mixed = call(
-        north_pole, jax.ShapeDtypeStruct((LAT, LON, WIDTH), BF),
+        second_pole, jax.ShapeDtypeStruct((LAT, LON, WIDTH), BF),
         work + [pltpu.VMEM((SHIFT, LON, WIDTH), BF), pltpu.SemaphoreType.DMA((3,))], 2_000_000_000,
-        pole_mask, raw, queries, pairs, from_north, part, low, gain, w_qkv, w_out, smem=1, in_hbm=True,
+        pole_mask, raw, queries, pairs, met_second, part, early, gain, w_qkv, w_out, smem=1, in_hbm=True,
     )
     return jnp.transpose(mixed, (1, 0, 2))
 

time: 35.7 us -> 35 us (0.980)
  the two profiles are of different devices: /device:TPU:2 before, /device:TPU:4 now
where the time goes in v4:
time: 35 us; the launch traced here: 34.8 us
  starting transfers between devices  21.3 us (61%)
  Pallas kernels  11.7 us (33%)
  local copies, waits for them, and re-layouts  1.18 us (3%)
  waiting for transfers between devices  0.44 us (1%)
    ppermute x1, starting transfers between devices, shards(): from_east = lax.ppermute(west, 'lon', [(b, a) for a, b in eastward])  13.5 us
    pallas_call x8, Pallas kernels, call(): pl.pallas_call(body, out_shape=out_shape, in_specs=specs, out_specs=jax.t...  11.7 us
    ppermute x1, starting transfers between devices, shards(): lax.ppermute(second, 'lat', [pair for a, b in northward[1::2] for pair in...  3.22 us
    ppermute x1, starting transfers between devices, shards(): lax.ppermute(first, 'lat', [pair for a, b in northward[0::2] for pair in...  2.59 us
    ppermute x1, starting transfers between devices, shards(): from_west = lax.ppermute(east, 'lon', eastward)  2.05 us
    unnamed x10, local copies, waits for them, and re-layouts  1.18 us
  transfers between devices with their start and end apart: 4, of which 1 were waited for; matrix products, arithmetic and copies ran while one was open for 0% of the time, Pallas kernels for 25%

profile of v4, /device:TPU:4, one launch (start us, length us, event | category | flops | bytes accessed | tf_op | source)
XLA Modules:
  0.0 34.8 jit_solution(11100272969683833500)
XLA Ops:
  0.0 0.0 copy-start.1
  0.0 1.2 %copy-done.1 = bf16[24,36,512]{2,0,1:T(8,128)(2,1)S(1)} copy-done((bf16[24,36,512]{2,0,1:T(8,128)(2,1)S(1)}, bf16[24,36,512]{2,0,1:T(8,128)(2,1)}, u32[]{:S(2)}) %copy-start.1) | copy-done | bytes 884760
  1.2 0.0 copy-start
  1.2 0.0 copy-start.2
  1.2 0.0 copy-start.3
  1.2 0.1 shard_map.56
  1.3 2.1 %collective-permute-start = (bf16[216,512]{1,0:T(8,128)(2,1)S(1)}, bf16[216,512]{1,0:T(8,128)(2,1)S(1)}, u32[]{:S(2)}, u32[]{:S(2)}) collective-permute-start(bf16[216,512]{1,0:T(8,128)(2,1)S(1)} %get-tuple-element.21), channel_id=1, source_target_pairs={{0,8},{8,16},{16,24},{24,32},{32,40},{40,48},{48,56},{56,64},{64,7... | collective-permute-start | bytes 663560 | tf_op jit(solution)/shard_map/ppermute | solution.py:300
  3.4 13.5 %collective-permute-start.1 = (bf16[216,512]{1,0:T(8,128)(2,1)S(1)}, bf16[216,512]{1,0:T(8,128)(2,1)S(1)}, u32[]{:S(2)}, u32[]{:S(2)}) collective-permute-start(bf16[216,512]{1,0:T(8,128)(2,1)S(1)} %get-tuple-element.24), channel_id=1, source_target_pairs={{8,0},{16,8},{24,16},{32,24},{40,32},{48,40},{56,48},{64,56},{72,6... | collective-permute-start | bytes 663560 | tf_op jit(solution)/shard_map/ppermute | solution.py:301
  16.9 0.0 copy-done
  16.9 0.0 copy-done.2
  16.9 0.0 copy-done.3
  16.9 2.0 %shard_map.55.refs_2_ = bf16[24,24,512]{2,1,0:T(8,128)(2,1)S(1)} custom-call(bf16[36,24,512]{2,1,0:T(8,128)(2,1)S(1)} %bitcast.4, f32[1,512]{1,0:T(1,128)S(1)} %bitcast.9, bf16[512,1536]{1,0:T(8,128)(2,1)S(1)} %copy-done, bf16[512,512]{1,0:T(8,128)(2,1)S(1)} %copy-done.2), custom_call_target="tpu_custom_call" | custom-call | flops 2000000000 | bytes 2000000 | tf_op jit(solution)/shard_map/pallas_call | solution.py:277
  18.9 0.0 collective-permute-done.refs_1_.from_west
  18.9 1.6 %shard_map.57.refs_2_ = bf16[24,24,512]{2,1,0:T(8,128)(2,1)S(1)} custom-call(bf16[36,24,512]{2,1,0:T(8,128)(2,1)S(1)} %bitcast.5, bf16[216,512]{1,0:T(8,128)(2,1)S(1)} %collective-permute-done.refs_1_.from_west, bf16[24,24,512]{2,1,0:T(8,128)(2,1)S(1)} %shard_map.55.refs_2_, f32[1,512]{1,0:T(1,128)S(1)} %bitcast.10, bf16[512,1536]{1,0:T(8,128)(2,1)S(1)} %copy-done, ...), custom_call_target="tpu_custom_call" | custom-call | flops 1000000 | bytes 1000 | tf_op jit(solution)/shard_map/pallas_call | solution.py:277
  20.6 0.0 collective-permute-done.1.from_east.refs_1_
  20.6 0.1 shard_map.60
  20.6 2.6 %collective-permute-start.2 = (bf16[216,512]{1,0:T(8,128)(2,1)S(1)}, bf16[216,512]{1,0:T(8,128)(2,1)S(1)}, u32[]{:S(2)}, u32[]{:S(2)}) collective-permute-start(bf16[216,512]{1,0:T(8,128)(2,1)S(1)} %get-tuple-element.31), channel_id=1, source_target_pairs={{0,1},{1,0},{2,3},{3,2},{4,5},{5,4},{6,7},{7,6},{8,9},{9,8},{10,11... | collective-permute-start | bytes 663560 | tf_op jit(solution)/shard_map/ppermute | solution.py:308
  23.2 3.2 %collective-permute-start.3 = (bf16[216,512]{1,0:T(8,128)(2,1)S(1)}, bf16[216,512]{1,0:T(8,128)(2,1)S(1)}, u32[]{:S(2)}, u32[]{:S(2)}) collective-permute-start(bf16[216,512]{1,0:T(8,128)(2,1)S(1)} %get-tuple-element.33), channel_id=1, source_target_pairs={{1,2},{2,1},{3,4},{4,3},{5,6},{6,5},{9,10},{10,9},{11,12},{12,11},... | collective-permute-start | bytes 663560 | tf_op jit(solution)/shard_map/ppermute | solution.py:309
  26.5 1.3 %shard_map.58 = (bf16[480,512]{1,0:T(8,128)(2,1)S(1)}, bf16[480,512]{1,0:T(8,128)(2,1)S(1)}, bf16[480,1024]{1,0:T(8,128)(2,1)S(1)}) custom-call(bf16[36,24,512]{2,1,0:T(8,128)(2,1)S(1)} %bitcast.7, bf16[216,512]{1,0:T(8,128)(2,1)S(1)} %collective-permute-done.refs_1_.from_west, bf16[216,512]{1,0:T(8,128)(2,1)S(1)} %collective-permute-done.1.from_east.refs_1_, ...), custom_call_target="tpu_custom_call" | custom-call | flops 1000000 | bytes 1000 | tf_op jit(solution)/shard_map/pallas_call | solution.py:277
  27.7 0.0 copy-start.4
  27.8 1.6 %shard_map.59.inner = bf16[24,24,512]{2,1,0:T(8,128)(2,1)S(1)} custom-call(bf16[36,24,512]{2,1,0:T(8,128)(2,1)S(1)} %bitcast.8, bf16[216,512]{1,0:T(8,128)(2,1)S(1)} %collective-permute-done.1.from_east.refs_1_, bf16[24,24,512]{2,1,0:T(8,128)(2,1)S(1)} %shard_map.57.refs_2_, f32[1,512]{1,0:T(1,128)S(1)} %bitcast.12, bf16[512,1536]{1,0:T(8,128)(2,1)S(1)} %copy-done, ...), custom_call_target="tpu_custom_call" | custom-call | flops 1000000 | bytes 1000 | tf_op jit(solution)/shard_map/pallas_call | solution.py:277
  29.4 0.0 collective-permute-done.2.refs_4_
  29.4 0.0 copy-done.4
  29.4 2.1 %shard_map.61.early = bf16[6,24,512]{2,1,0:T(8,128)(2,1)S(1)} custom-call(s32[288]{0:T(512)S(1)} %copy-done.4, bf16[480,512]{1,0:T(8,128)(2,1)S(1)} %get-tuple-element.27.refs_1_.raw, bf16[480,512]{1,0:T(8,128)(2,1)S(1)} %get-tuple-element.28.refs_2_.queries, bf16[480,1024]{1,0:T(8,128)(2,1)S(1)} %get-tuple-element.29.refs_3_.own_pairs, ...), custom_call_target="tpu_custom_call" | custom-call | flops 1000000 | bytes 1000 | tf_op jit(solution)/shard_map/pallas_call | solution.py:277
  31.5 0.4 %collective-permute-done.3.arrived = bf16[216,512]{1,0:T(8,128)(2,1)S(1)} collective-permute-done((bf16[216,512]{1,0:T(8,128)(2,1)S(1)}, bf16[216,512]{1,0:T(8,128)(2,1)S(1)}, u32[]{:S(2)}, u32[]{:S(2)}) %collective-permute-start.3) | collective-permute-done | bytes 221216 | tf_op jit(solution)/shard_map/ppermute | solution.py:309
  32.0 2.8 %shard_map.62 = bf16[36,24,512]{2,1,0:T(8,128)(2,1)} custom-call(s32[288]{0:T(512)S(1)} %copy-done.4, bf16[480,512]{1,0:T(8,128)(2,1)S(1)} %get-tuple-element.27.refs_1_.raw, bf16[480,512]{1,0:T(8,128)(2,1)S(1)} %get-tuple-element.28.refs_2_.queries, bf16[480,1024]{1,0:T(8,128)(2,1)S(1)} %get-tuple-element.29.refs_3_.own_pairs, ...), custom_call_target="tpu_custom_call" | custom-call | flops 2000000000 | bytes 2000000 | tf_op jit(solution)/shard_map/pallas_call | solution.py:277
Async XLA Ops:
  0.0 1.2 %copy-start.1 = (bf16[24,36,512]{2,0,1:T(8,128)(2,1)S(1)}, bf16[24,36,512]{2,0,1:T(8,128)(2,1)}, u32[]{:S(2)}) copy-start(bf16[24,36,512]{2,0,1:T(8,128)(2,1)} %param.5) | copy-start | bytes 2654212
  1.2 15.7 %copy-start = (bf16[512,1536]{1,0:T(8,128)(2,1)S(1)}, bf16[512,1536]{1,0:T(8,128)(2,1)}, u32[]{:S(2)}) copy-start(bf16[512,1536]{1,0:T(8,128)(2,1)} %w_qkv.5) | copy-start | bytes 4718596
  1.2 15.7 %copy-start.2 = (bf16[512,512]{1,0:T(8,128)(2,1)S(1)}, bf16[512,512]{1,0:T(8,128)(2,1)}, u32[]{:S(2)}) copy-start(bf16[512,512]{1,0:T(8,128)(2,1)} %w_out.3) | copy-start | bytes 1572868
  1.2 15.7 %copy-start.3 = (f32[512]{0:T(512)S(1)}, f32[512]{0:T(512)}, u32[]{:S(2)}) copy-start(f32[512]{0:T(512)} %param.6) | copy-start | bytes 6148
  1.3 17.6 %collective-permute-start = (bf16[216,512]{1,0:T(8,128)(2,1)S(1)}, bf16[216,512]{1,0:T(8,128)(2,1)S(1)}, u32[]{:S(2)}, u32[]{:S(2)}) collective-permute-start(bf16[216,512]{1,0:T(8,128)(2,1)S(1)} %get-tuple-element.21), channel_id=1, source_target_pairs={{0,8},{8,16},{16,24},{24,32},{32,40},{40,48},{48,56},{56,64},{64,7... | collective-permute-start | bytes 663560 | tf_op jit(solution)/shard_map/ppermute | solution.py:300
  3.4 17.2 %collective-permute-start.1 = (bf16[216,512]{1,0:T(8,128)(2,1)S(1)}, bf16[216,512]{1,0:T(8,128)(2,1)S(1)}, u32[]{:S(2)}, u32[]{:S(2)}) collective-permute-start(bf16[216,512]{1,0:T(8,128)(2,1)S(1)} %get-tuple-element.24), channel_id=1, source_target_pairs={{8,0},{16,8},{24,16},{32,24},{40,32},{48,40},{56,48},{64,56},{72,6... | collective-permute-start | bytes 663560 | tf_op jit(solution)/shard_map/ppermute | solution.py:301
  20.6 8.8 %collective-permute-start.2 = (bf16[216,512]{1,0:T(8,128)(2,1)S(1)}, bf16[216,512]{1,0:T(8,128)(2,1)S(1)}, u32[]{:S(2)}, u32[]{:S(2)}) collective-permute-start(bf16[216,512]{1,0:T(8,128)(2,1)S(1)} %get-tuple-element.31), channel_id=1, source_target_pairs={{0,1},{1,0},{2,3},{3,2},{4,5},{5,4},{6,7},{7,6},{8,9},{9,8},{10,11... | collective-permute-start | bytes 663560 | tf_op jit(solution)/shard_map/ppermute | solution.py:308
  23.2 8.7 %collective-permute-start.3 = (bf16[216,512]{1,0:T(8,128)(2,1)S(1)}, bf16[216,512]{1,0:T(8,128)(2,1)S(1)}, u32[]{:S(2)}, u32[]{:S(2)}) collective-permute-start(bf16[216,512]{1,0:T(8,128)(2,1)S(1)} %get-tuple-element.33), channel_id=1, source_target_pairs={{1,2},{2,1},{3,4},{4,3},{5,6},{6,5},{9,10},{10,9},{11,12},{12,11},... | collective-permute-start | bytes 663560 | tf_op jit(solution)/shard_map/ppermute | solution.py:309
  27.7 1.7 %copy-start.4 = (s32[288]{0:T(512)S(1)}, s32[288]{0:T(512)}, u32[]{:S(2)}) copy-start(s32[288]{0:T(512)} %mask.1) | copy-start | bytes 3460

commit v5 on v4

--- a/solution.py
+++ b/solution.py
@@ -209,7 +209,7 @@
 
 def pole_windows(
     north, mask, raw, queries, own_pairs, arrived, gain, w_qkv, w_out, result,
-    halo, stack, normed, pairs, context, mixed, x32,
+    halo, stack, normed, pairs, context, mixed, x32, copies=(),
 ):
     halo[...] = arrived[...].astype(F32)
     for step in range(SHIFT):
@@ -229,12 +229,17 @@
         at = HALF * index
         parts = [(own_pairs, base + at, HALF), (pairs, at, HALF)]
         window_context(queries, base + at, at, HALF, parts, context, bias)
-    finish(context, w_out, raw, base, HALF, HALF, mixed)
-    for step in range(SHIFT):
-        x32[step, 6:18, :] = mixed[12 * step : 12 * step + 12, :]
-        x32[step, 0:6, :] = mixed[80 + 6 * step : 86 + 6 * step, :]
-        x32[step, 18:24, :] = mixed[160 + 6 * step : 166 + 6 * step, :]
-    result[...] = x32[...].astype(BF)
+    for col in range(0, WIDTH, 256):
+        cols = slice(col, col + 256)
+        part = jnp.dot(context[...], w_out[:, cols], preferred_element_type=F32)
+        mixed[:, cols] = part + raw[pl.ds(base, 3 * HALF), cols].astype(F32)
+        for step in range(SHIFT):
+            x32[step, 6:18, cols] = mixed[12 * step : 12 * step + 12, cols]
+            x32[step, 0:6, cols] = mixed[80 + 6 * step : 86 + 6 * step, cols]
+            x32[step, 18:24, cols] = mixed[160 + 6 * step : 166 + 6 * step, cols]
+        result[:, :, cols] = x32[:, :, cols].astype(BF)
+        if copies:
+            copies[col // 256].start()
 
 
 def first_pole(*refs):
@@ -248,12 +253,16 @@
     copies = [
         pltpu.make_async_copy(inner, out.at[SHIFT : LAT - SHIFT], sem.at[0]),
         pltpu.make_async_copy(early, out.at[pl.ds(far - far * north, SHIFT)], sem.at[1]),
-        pltpu.make_async_copy(rows, out.at[pl.ds(far * north, SHIFT)], sem.at[2]),
+        *(
+            pltpu.make_async_copy(
+                rows.at[:, :, pl.ds(col, 256)], out.at[pl.ds(far * north, SHIFT), :, pl.ds(col, 256)], sem.at[2 + col // 256]
+            )
+            for col in range(0, WIDTH, 256)
+        ),
     ]
     copies[0].start()
     copies[1].start()
-    pole_windows(north, mask, raw, queries, own_pairs, arrived, gain, w_qkv, w_out, rows, *work)
-    copies[2].start()
+    pole_windows(north, mask, raw, queries, own_pairs, arrived, gain, w_qkv, w_out, rows, *work, copies=copies[2:])
     for copy in copies:
         copy.wait()
 
@@ -325,7 +334,7 @@
     early, met_second = lax.optimization_barrier((early, met_second))
     mixed = call(
         second_pole, jax.ShapeDtypeStruct((LAT, LON, WIDTH), BF),
-        work + [pltpu.VMEM((SHIFT, LON, WIDTH), BF), pltpu.SemaphoreType.DMA((3,))], 2_000_000_000,
+        work + [pltpu.VMEM((SHIFT, LON, WIDTH), BF), pltpu.SemaphoreType.DMA((4,))], 2_000_000_000,
         pole_mask, raw, queries, pairs, met_second, part, early, gain, w_qkv, w_out, smem=1, in_hbm=True,
     )
     return jnp.transpose(mixed, (1, 0, 2))

time: 35 us -> 35 us (level)
  the two profiles are of different devices: /device:TPU:4 before, /device:TPU:2 now
where the time goes in v5:
time: 35 us; the launch traced here: 34.8 us
  starting transfers between devices  21.3 us (61%)
  Pallas kernels  11.7 us (33%)
  local copies, waits for them, and re-layouts  1.18 us (3%)
  waiting for transfers between devices  0.43 us (1%)
    ppermute x1, starting transfers between devices, shards(): from_east = lax.ppermute(west, 'lon', [(b, a) for a, b in eastward])  13.5 us
    pallas_call x8, Pallas kernels, call(): pl.pallas_call(body, out_shape=out_shape, in_specs=specs, out_specs=jax.t...  11.7 us
    ppermute x1, starting transfers between devices, shards(): lax.ppermute(second, 'lat', [pair for a, b in northward[1::2] for pair in...  3.23 us
    ppermute x1, starting transfers between devices, shards(): lax.ppermute(first, 'lat', [pair for a, b in northward[0::2] for pair in...  2.59 us
    ppermute x1, starting transfers between devices, shards(): from_west = lax.ppermute(east, 'lon', eastward)  2.05 us
    unnamed x10, local copies, waits for them, and re-layouts  1.18 us
  transfers between devices with their start and end apart: 4, of which 1 were waited for; matrix products, arithmetic and copies ran while one was open for 0% of the time, Pallas kernels for 25%

profile of v5, /device:TPU:2, one launch (start us, length us, event | category | flops | bytes accessed | tf_op | source)
XLA Modules:
  0.0 34.8 jit_solution(6256842041635435090)
XLA Ops:
  0.0 0.0 copy-start.1
  0.0 1.2 %copy-done.1 = bf16[24,36,512]{2,0,1:T(8,128)(2,1)S(1)} copy-done((bf16[24,36,512]{2,0,1:T(8,128)(2,1)S(1)}, bf16[24,36,512]{2,0,1:T(8,128)(2,1)}, u32[]{:S(2)}) %copy-start.1) | copy-done | bytes 884760
  1.2 0.0 copy-start
  1.2 0.0 copy-start.2
  1.2 0.0 copy-start.3
  1.2 0.1 shard_map.56
  1.3 2.1 %collective-permute-start = (bf16[216,512]{1,0:T(8,128)(2,1)S(1)}, bf16[216,512]{1,0:T(8,128)(2,1)S(1)}, u32[]{:S(2)}, u32[]{:S(2)}) collective-permute-start(bf16[216,512]{1,0:T(8,128)(2,1)S(1)} %get-tuple-element.21), channel_id=1, source_target_pairs={{0,8},{8,16},{16,24},{24,32},{32,40},{40,48},{48,56},{56,64},{64,7... | collective-permute-start | bytes 663560 | tf_op jit(solution)/shard_map/ppermute | solution.py:309
  3.4 13.5 %collective-permute-start.1 = (bf16[216,512]{1,0:T(8,128)(2,1)S(1)}, bf16[216,512]{1,0:T(8,128)(2,1)S(1)}, u32[]{:S(2)}, u32[]{:S(2)}) collective-permute-start(bf16[216,512]{1,0:T(8,128)(2,1)S(1)} %get-tuple-element.24), channel_id=1, source_target_pairs={{8,0},{16,8},{24,16},{32,24},{40,32},{48,40},{56,48},{64,56},{72,6... | collective-permute-start | bytes 663560 | tf_op jit(solution)/shard_map/ppermute | solution.py:310
  16.9 0.0 copy-done
  16.9 0.0 copy-done.2
  16.9 0.0 copy-done.3
  16.9 2.0 %shard_map.55.refs_2_ = bf16[24,24,512]{2,1,0:T(8,128)(2,1)S(1)} custom-call(bf16[36,24,512]{2,1,0:T(8,128)(2,1)S(1)} %bitcast.4, f32[1,512]{1,0:T(1,128)S(1)} %bitcast.9, bf16[512,1536]{1,0:T(8,128)(2,1)S(1)} %copy-done, bf16[512,512]{1,0:T(8,128)(2,1)S(1)} %copy-done.2), custom_call_target="tpu_custom_call" | custom-call | flops 2000000000 | bytes 2000000 | tf_op jit(solution)/shard_map/pallas_call | solution.py:286
  18.9 0.0 collective-permute-done.refs_1_.from_west
  18.9 1.6 %shard_map.57.refs_2_ = bf16[24,24,512]{2,1,0:T(8,128)(2,1)S(1)} custom-call(bf16[36,24,512]{2,1,0:T(8,128)(2,1)S(1)} %bitcast.5, bf16[216,512]{1,0:T(8,128)(2,1)S(1)} %collective-permute-done.refs_1_.from_west, bf16[24,24,512]{2,1,0:T(8,128)(2,1)S(1)} %shard_map.55.refs_2_, f32[1,512]{1,0:T(1,128)S(1)} %bitcast.10, bf16[512,1536]{1,0:T(8,128)(2,1)S(1)} %copy-done, ...), custom_call_target="tpu_custom_call" | custom-call | flops 1000000 | bytes 1000 | tf_op jit(solution)/shard_map/pallas_call | solution.py:286
  20.6 0.0 collective-permute-done.1.from_east.refs_1_
  20.6 0.1 shard_map.60
  20.6 2.6 %collective-permute-start.2 = (bf16[216,512]{1,0:T(8,128)(2,1)S(1)}, bf16[216,512]{1,0:T(8,128)(2,1)S(1)}, u32[]{:S(2)}, u32[]{:S(2)}) collective-permute-start(bf16[216,512]{1,0:T(8,128)(2,1)S(1)} %get-tuple-element.31), channel_id=1, source_target_pairs={{0,1},{1,0},{2,3},{3,2},{4,5},{5,4},{6,7},{7,6},{8,9},{9,8},{10,11... | collective-permute-start | bytes 663560 | tf_op jit(solution)/shard_map/ppermute | solution.py:317
  23.2 3.2 %collective-permute-start.3 = (bf16[216,512]{1,0:T(8,128)(2,1)S(1)}, bf16[216,512]{1,0:T(8,128)(2,1)S(1)}, u32[]{:S(2)}, u32[]{:S(2)}) collective-permute-start(bf16[216,512]{1,0:T(8,128)(2,1)S(1)} %get-tuple-element.33), channel_id=1, source_target_pairs={{1,2},{2,1},{3,4},{4,3},{5,6},{6,5},{9,10},{10,9},{11,12},{12,11},... | collective-permute-start | bytes 663560 | tf_op jit(solution)/shard_map/ppermute | solution.py:318
  26.5 1.3 %shard_map.58 = (bf16[480,512]{1,0:T(8,128)(2,1)S(1)}, bf16[480,512]{1,0:T(8,128)(2,1)S(1)}, bf16[480,1024]{1,0:T(8,128)(2,1)S(1)}) custom-call(bf16[36,24,512]{2,1,0:T(8,128)(2,1)S(1)} %bitcast.7, bf16[216,512]{1,0:T(8,128)(2,1)S(1)} %collective-permute-done.refs_1_.from_west, bf16[216,512]{1,0:T(8,128)(2,1)S(1)} %collective-permute-done.1.from_east.refs_1_, ...), custom_call_target="tpu_custom_call" | custom-call | flops 1000000 | bytes 1000 | tf_op jit(solution)/shard_map/pallas_call | solution.py:286
  27.7 0.0 copy-start.4
  27.8 1.6 %shard_map.59.inner = bf16[24,24,512]{2,1,0:T(8,128)(2,1)S(1)} custom-call(bf16[36,24,512]{2,1,0:T(8,128)(2,1)S(1)} %bitcast.8, bf16[216,512]{1,0:T(8,128)(2,1)S(1)} %collective-permute-done.1.from_east.refs_1_, bf16[24,24,512]{2,1,0:T(8,128)(2,1)S(1)} %shard_map.57.refs_2_, f32[1,512]{1,0:T(1,128)S(1)} %bitcast.12, bf16[512,1536]{1,0:T(8,128)(2,1)S(1)} %copy-done, ...), custom_call_target="tpu_custom_call" | custom-call | flops 1000000 | bytes 1000 | tf_op jit(solution)/shard_map/pallas_call | solution.py:286
  29.4 0.0 collective-permute-done.2.refs_4_
  29.4 0.0 copy-done.4
  29.4 2.1 %shard_map.61.early = bf16[6,24,512]{2,1,0:T(8,128)(2,1)S(1)} custom-call(s32[288]{0:T(512)S(1)} %copy-done.4, bf16[480,512]{1,0:T(8,128)(2,1)S(1)} %get-tuple-element.27.refs_1_.raw, bf16[480,512]{1,0:T(8,128)(2,1)S(1)} %get-tuple-element.28.refs_2_.queries, bf16[480,1024]{1,0:T(8,128)(2,1)S(1)} %get-tuple-element.29.refs_3_.own_pairs, ...), custom_call_target="tpu_custom_call" | custom-call | flops 1000000 | bytes 1000 | tf_op jit(solution)/shard_map/pallas_call | solution.py:286
  31.5 0.4 %collective-permute-done.3.arrived = bf16[216,512]{1,0:T(8,128)(2,1)S(1)} collective-permute-done((bf16[216,512]{1,0:T(8,128)(2,1)S(1)}, bf16[216,512]{1,0:T(8,128)(2,1)S(1)}, u32[]{:S(2)}, u32[]{:S(2)}) %collective-permute-start.3) | collective-permute-done | bytes 221216 | tf_op jit(solution)/shard_map/ppermute | solution.py:318
  32.0 2.8 %shard_map.62 = bf16[36,24,512]{2,1,0:T(8,128)(2,1)} custom-call(s32[288]{0:T(512)S(1)} %copy-done.4, bf16[480,512]{1,0:T(8,128)(2,1)S(1)} %get-tuple-element.27.refs_1_.raw, bf16[480,512]{1,0:T(8,128)(2,1)S(1)} %get-tuple-element.28.refs_2_.queries, bf16[480,1024]{1,0:T(8,128)(2,1)S(1)} %get-tuple-element.29.refs_3_.own_pairs, ...), custom_call_target="tpu_custom_call" | custom-call | flops 2000000000 | bytes 2000000 | tf_op jit(solution)/shard_map/pallas_call | solution.py:286
Async XLA Ops:
  0.0 1.2 %copy-start.1 = (bf16[24,36,512]{2,0,1:T(8,128)(2,1)S(1)}, bf16[24,36,512]{2,0,1:T(8,128)(2,1)}, u32[]{:S(2)}) copy-start(bf16[24,36,512]{2,0,1:T(8,128)(2,1)} %param.5) | copy-start | bytes 2654212
  1.2 15.7 %copy-start = (bf16[512,1536]{1,0:T(8,128)(2,1)S(1)}, bf16[512,1536]{1,0:T(8,128)(2,1)}, u32[]{:S(2)}) copy-start(bf16[512,1536]{1,0:T(8,128)(2,1)} %w_qkv.5) | copy-start | bytes 4718596
  1.2 15.7 %copy-start.2 = (bf16[512,512]{1,0:T(8,128)(2,1)S(1)}, bf16[512,512]{1,0:T(8,128)(2,1)}, u32[]{:S(2)}) copy-start(bf16[512,512]{1,0:T(8,128)(2,1)} %w_out.3) | copy-start | bytes 1572868
  1.2 15.7 %copy-start.3 = (f32[512]{0:T(512)S(1)}, f32[512]{0:T(512)}, u32[]{:S(2)}) copy-start(f32[512]{0:T(512)} %param.6) | copy-start | bytes 6148
  1.3 17.6 %collective-permute-start = (bf16[216,512]{1,0:T(8,128)(2,1)S(1)}, bf16[216,512]{1,0:T(8,128)(2,1)S(1)}, u32[]{:S(2)}, u32[]{:S(2)}) collective-permute-start(bf16[216,512]{1,0:T(8,128)(2,1)S(1)} %get-tuple-element.21), channel_id=1, source_target_pairs={{0,8},{8,16},{16,24},{24,32},{32,40},{40,48},{48,56},{56,64},{64,7... | collective-permute-start | bytes 663560 | tf_op jit(solution)/shard_map/ppermute | solution.py:309
  3.4 17.2 %collective-permute-start.1 = (bf16[216,512]{1,0:T(8,128)(2,1)S(1)}, bf16[216,512]{1,0:T(8,128)(2,1)S(1)}, u32[]{:S(2)}, u32[]{:S(2)}) collective-permute-start(bf16[216,512]{1,0:T(8,128)(2,1)S(1)} %get-tuple-element.24), channel_id=1, source_target_pairs={{8,0},{16,8},{24,16},{32,24},{40,32},{48,40},{56,48},{64,56},{72,6... | collective-permute-start | bytes 663560 | tf_op jit(solution)/shard_map/ppermute | solution.py:310
  20.6 8.8 %collective-permute-start.2 = (bf16[216,512]{1,0:T(8,128)(2,1)S(1)}, bf16[216,512]{1,0:T(8,128)(2,1)S(1)}, u32[]{:S(2)}, u32[]{:S(2)}) collective-permute-start(bf16[216,512]{1,0:T(8,128)(2,1)S(1)} %get-tuple-element.31), channel_id=1, source_target_pairs={{0,1},{1,0},{2,3},{3,2},{4,5},{5,4},{6,7},{7,6},{8,9},{9,8},{10,11... | collective-permute-start | bytes 663560 | tf_op jit(solution)/shard_map/ppermute | solution.py:317
  23.2 8.7 %collective-permute-start.3 = (bf16[216,512]{1,0:T(8,128)(2,1)S(1)}, bf16[216,512]{1,0:T(8,128)(2,1)S(1)}, u32[]{:S(2)}, u32[]{:S(2)}) collective-permute-start(bf16[216,512]{1,0:T(8,128)(2,1)S(1)} %get-tuple-element.33), channel_id=1, source_target_pairs={{1,2},{2,1},{3,4},{4,3},{5,6},{6,5},{9,10},{10,9},{11,12},{12,11},... | collective-permute-start | bytes 663560 | tf_op jit(solution)/shard_map/ppermute | solution.py:318
  27.7 1.7 %copy-start.4 = (s32[288]{0:T(512)S(1)}, s32[288]{0:T(512)}, u32[]{:S(2)}) copy-start(s32[288]{0:T(512)} %mask.1) | copy-start | bytes 3460

commit v6 on v4

--- a/solution.py
+++ b/solution.py
@@ -127,9 +127,8 @@
 
 
 def middle(x, gain, w_qkv, w_out, out, x32, stack, normed, q_rows, pairs, queries, context, mixed):
-    x32[...] = x[SHIFT : LAT - SHIFT].astype(F32)
     for lat in range(24):
-        stack[12 * lat : 12 * lat + 12, :] = x32[lat, 6:18, :]
+        stack[12 * lat : 12 * lat + 12, :] = x[SHIFT + lat].astype(F32)[6:18]
     attend(stack, gain, w_qkv, w_out, KEYS, normed, q_rows, pairs, queries, context, mixed)
     for lat in range(24):
         x32[lat, 6:18, :] = mixed[12 * lat : 12 * lat + 12, :]
@@ -138,12 +137,11 @@
 
 def side_windows(east, x, halo, done, gain, w_qkv, w_out, out, x32, halo32, stack, normed, q_rows, pairs, queries, context, mixed):
     lon = LON - SHIFT if east else 0
-    x32[...] = x[SHIFT : LAT - SHIFT].astype(F32)
     halo32[...] = halo[...].astype(F32)
     for band in range(2):
         base = KEYS * band
         for step in range(12):
-            stack[base + 6 * step : base + 6 * step + 6, :] = x32[12 * band + step, lon : lon + 6, :]
+            stack[base + 6 * step : base + 6 * step + 6, :] = x[SHIFT + 12 * band + step].astype(F32)[lon : lon + 6]
         stack[base + 72 : base + 144, :] = halo32[36 + 72 * band : 108 + 72 * band, :]
     attend(stack, gain, w_qkv, w_out, HALF, normed, q_rows, pairs, queries, context, mixed)
     x32[...] = done[...].astype(F32)

time: 35 us -> 34.9 us (level)
  the two profiles are of different devices: /device:TPU:4 before, /device:TPU:2 now
where the time goes in v6:
time: 34.9 us; the launch traced here: 34.7 us
  starting transfers between devices  21.3 us (61%)
  Pallas kernels  11.6 us (33%)
  local copies, waits for them, and re-layouts  1.18 us (3%)
  waiting for transfers between devices  0.44 us (1%)
    ppermute x1, starting transfers between devices, shards(): from_east = lax.ppermute(west, 'lon', [(b, a) for a, b in eastward])  13.5 us
    pallas_call x8, Pallas kernels, call(): pl.pallas_call(body, out_shape=out_shape, in_specs=specs, out_specs=jax.t...  11.6 us
    ppermute x1, starting transfers between devices, shards(): lax.ppermute(second, 'lat', [pair for a, b in northward[1::2] for pair in...  3.22 us
    ppermute x1, starting transfers between devices, shards(): lax.ppermute(first, 'lat', [pair for a, b in northward[0::2] for pair in...  2.58 us
    ppermute x1, starting transfers between devices, shards(): from_west = lax.ppermute(east, 'lon', eastward)  2.05 us
    unnamed x10, local copies, waits for them, and re-layouts  1.18 us
  transfers between devices with their start and end apart: 4, of which 1 were waited for; matrix products, arithmetic and copies ran while one was open for 0% of the time, Pallas kernels for 25%

profile of v6, /device:TPU:2, one launch (start us, length us, event | category | flops | bytes accessed | tf_op | source)
XLA Modules:
  0.0 34.7 jit_solution(9708969206994578329)
XLA Ops:
  0.0 0.0 copy-start.1
  0.0 1.2 %copy-done.1 = bf16[24,36,512]{2,0,1:T(8,128)(2,1)S(1)} copy-done((bf16[24,36,512]{2,0,1:T(8,128)(2,1)S(1)}, bf16[24,36,512]{2,0,1:T(8,128)(2,1)}, u32[]{:S(2)}) %copy-start.1) | copy-done | bytes 884760
  1.2 0.0 copy-start
  1.2 0.0 copy-start.2
  1.2 0.0 copy-start.3
  1.2 0.1 shard_map.56
  1.3 2.1 %collective-permute-start = (bf16[216,512]{1,0:T(8,128)(2,1)S(1)}, bf16[216,512]{1,0:T(8,128)(2,1)S(1)}, u32[]{:S(2)}, u32[]{:S(2)}) collective-permute-start(bf16[216,512]{1,0:T(8,128)(2,1)S(1)} %get-tuple-element.21), channel_id=1, source_target_pairs={{0,8},{8,16},{16,24},{24,32},{32,40},{40,48},{48,56},{56,64},{64,7... | collective-permute-start | bytes 663560 | tf_op jit(solution)/shard_map/ppermute | solution.py:298
  3.4 13.5 %collective-permute-start.1 = (bf16[216,512]{1,0:T(8,128)(2,1)S(1)}, bf16[216,512]{1,0:T(8,128)(2,1)S(1)}, u32[]{:S(2)}, u32[]{:S(2)}) collective-permute-start(bf16[216,512]{1,0:T(8,128)(2,1)S(1)} %get-tuple-element.24), channel_id=1, source_target_pairs={{8,0},{16,8},{24,16},{32,24},{40,32},{48,40},{56,48},{64,56},{72,6... | collective-permute-start | bytes 663560 | tf_op jit(solution)/shard_map/ppermute | solution.py:299
  16.9 0.0 copy-done
  16.9 0.0 copy-done.2
  16.9 0.0 copy-done.3
  16.9 2.0 %shard_map.55.refs_2_ = bf16[24,24,512]{2,1,0:T(8,128)(2,1)S(1)} custom-call(bf16[36,24,512]{2,1,0:T(8,128)(2,1)S(1)} %bitcast.4, f32[1,512]{1,0:T(1,128)S(1)} %bitcast.9, bf16[512,1536]{1,0:T(8,128)(2,1)S(1)} %copy-done, bf16[512,512]{1,0:T(8,128)(2,1)S(1)} %copy-done.2), custom_call_target="tpu_custom_call" | custom-call | flops 2000000000 | bytes 2000000 | tf_op jit(solution)/shard_map/pallas_call | solution.py:275
  18.9 0.0 collective-permute-done.refs_1_.from_west
  18.9 1.6 %shard_map.57.refs_2_ = bf16[24,24,512]{2,1,0:T(8,128)(2,1)S(1)} custom-call(bf16[36,24,512]{2,1,0:T(8,128)(2,1)S(1)} %bitcast.5, bf16[216,512]{1,0:T(8,128)(2,1)S(1)} %collective-permute-done.refs_1_.from_west, bf16[24,24,512]{2,1,0:T(8,128)(2,1)S(1)} %shard_map.55.refs_2_, f32[1,512]{1,0:T(1,128)S(1)} %bitcast.10, bf16[512,1536]{1,0:T(8,128)(2,1)S(1)} %copy-done, ...), custom_call_target="tpu_custom_call" | custom-call | flops 1000000 | bytes 1000 | tf_op jit(solution)/shard_map/pallas_call | solution.py:275
  20.5 0.0 collective-permute-done.1.from_east.refs_1_
  20.5 0.1 shard_map.60
  20.6 2.6 %collective-permute-start.2 = (bf16[216,512]{1,0:T(8,128)(2,1)S(1)}, bf16[216,512]{1,0:T(8,128)(2,1)S(1)}, u32[]{:S(2)}, u32[]{:S(2)}) collective-permute-start(bf16[216,512]{1,0:T(8,128)(2,1)S(1)} %get-tuple-element.31), channel_id=1, source_target_pairs={{0,1},{1,0},{2,3},{3,2},{4,5},{5,4},{6,7},{7,6},{8,9},{9,8},{10,11... | collective-permute-start | bytes 663560 | tf_op jit(solution)/shard_map/ppermute | solution.py:306
  23.2 3.2 %collective-permute-start.3 = (bf16[216,512]{1,0:T(8,128)(2,1)S(1)}, bf16[216,512]{1,0:T(8,128)(2,1)S(1)}, u32[]{:S(2)}, u32[]{:S(2)}) collective-permute-start(bf16[216,512]{1,0:T(8,128)(2,1)S(1)} %get-tuple-element.33), channel_id=1, source_target_pairs={{1,2},{2,1},{3,4},{4,3},{5,6},{6,5},{9,10},{10,9},{11,12},{12,11},... | collective-permute-start | bytes 663560 | tf_op jit(solution)/shard_map/ppermute | solution.py:307
  26.4 1.3 %shard_map.58 = (bf16[480,512]{1,0:T(8,128)(2,1)S(1)}, bf16[480,512]{1,0:T(8,128)(2,1)S(1)}, bf16[480,1024]{1,0:T(8,128)(2,1)S(1)}) custom-call(bf16[36,24,512]{2,1,0:T(8,128)(2,1)S(1)} %bitcast.7, bf16[216,512]{1,0:T(8,128)(2,1)S(1)} %collective-permute-done.refs_1_.from_west, bf16[216,512]{1,0:T(8,128)(2,1)S(1)} %collective-permute-done.1.from_east.refs_1_, ...), custom_call_target="tpu_custom_call" | custom-call | flops 1000000 | bytes 1000 | tf_op jit(solution)/shard_map/pallas_call | solution.py:275
  27.7 0.0 copy-start.4
  27.7 1.6 %shard_map.59.inner = bf16[24,24,512]{2,1,0:T(8,128)(2,1)S(1)} custom-call(bf16[36,24,512]{2,1,0:T(8,128)(2,1)S(1)} %bitcast.8, bf16[216,512]{1,0:T(8,128)(2,1)S(1)} %collective-permute-done.1.from_east.refs_1_, bf16[24,24,512]{2,1,0:T(8,128)(2,1)S(1)} %shard_map.57.refs_2_, f32[1,512]{1,0:T(1,128)S(1)} %bitcast.12, bf16[512,1536]{1,0:T(8,128)(2,1)S(1)} %copy-done, ...), custom_call_target="tpu_custom_call" | custom-call | flops 1000000 | bytes 1000 | tf_op jit(solution)/shard_map/pallas_call | solution.py:275
  29.3 0.0 collective-permute-done.2.refs_4_
  29.3 0.0 copy-done.4
  29.4 2.1 %shard_map.61.early = bf16[6,24,512]{2,1,0:T(8,128)(2,1)S(1)} custom-call(s32[288]{0:T(512)S(1)} %copy-done.4, bf16[480,512]{1,0:T(8,128)(2,1)S(1)} %get-tuple-element.27.refs_1_.raw, bf16[480,512]{1,0:T(8,128)(2,1)S(1)} %get-tuple-element.28.refs_2_.queries, bf16[480,1024]{1,0:T(8,128)(2,1)S(1)} %get-tuple-element.29.refs_3_.own_pairs, ...), custom_call_target="tpu_custom_call" | custom-call | flops 1000000 | bytes 1000 | tf_op jit(solution)/shard_map/pallas_call | solution.py:275
  31.5 0.4 %collective-permute-done.3.arrived = bf16[216,512]{1,0:T(8,128)(2,1)S(1)} collective-permute-done((bf16[216,512]{1,0:T(8,128)(2,1)S(1)}, bf16[216,512]{1,0:T(8,128)(2,1)S(1)}, u32[]{:S(2)}, u32[]{:S(2)}) %collective-permute-start.3) | collective-permute-done | bytes 221216 | tf_op jit(solution)/shard_map/ppermute | solution.py:307
  31.9 2.8 %shard_map.62 = bf16[36,24,512]{2,1,0:T(8,128)(2,1)} custom-call(s32[288]{0:T(512)S(1)} %copy-done.4, bf16[480,512]{1,0:T(8,128)(2,1)S(1)} %get-tuple-element.27.refs_1_.raw, bf16[480,512]{1,0:T(8,128)(2,1)S(1)} %get-tuple-element.28.refs_2_.queries, bf16[480,1024]{1,0:T(8,128)(2,1)S(1)} %get-tuple-element.29.refs_3_.own_pairs, ...), custom_call_target="tpu_custom_call" | custom-call | flops 2000000000 | bytes 2000000 | tf_op jit(solution)/shard_map/pallas_call | solution.py:275
Async XLA Ops:
  0.0 1.2 %copy-start.1 = (bf16[24,36,512]{2,0,1:T(8,128)(2,1)S(1)}, bf16[24,36,512]{2,0,1:T(8,128)(2,1)}, u32[]{:S(2)}) copy-start(bf16[24,36,512]{2,0,1:T(8,128)(2,1)} %param.5) | copy-start | bytes 2654212
  1.2 15.7 %copy-start = (bf16[512,1536]{1,0:T(8,128)(2,1)S(1)}, bf16[512,1536]{1,0:T(8,128)(2,1)}, u32[]{:S(2)}) copy-start(bf16[512,1536]{1,0:T(8,128)(2,1)} %w_qkv.5) | copy-start | bytes 4718596
  1.2 15.7 %copy-start.2 = (bf16[512,512]{1,0:T(8,128)(2,1)S(1)}, bf16[512,512]{1,0:T(8,128)(2,1)}, u32[]{:S(2)}) copy-start(bf16[512,512]{1,0:T(8,128)(2,1)} %w_out.3) | copy-start | bytes 1572868
  1.2 15.7 %copy-start.3 = (f32[512]{0:T(512)S(1)}, f32[512]{0:T(512)}, u32[]{:S(2)}) copy-start(f32[512]{0:T(512)} %param.6) | copy-start | bytes 6148
  1.3 17.5 %collective-permute-start = (bf16[216,512]{1,0:T(8,128)(2,1)S(1)}, bf16[216,512]{1,0:T(8,128)(2,1)S(1)}, u32[]{:S(2)}, u32[]{:S(2)}) collective-permute-start(bf16[216,512]{1,0:T(8,128)(2,1)S(1)} %get-tuple-element.21), channel_id=1, source_target_pairs={{0,8},{8,16},{16,24},{24,32},{32,40},{40,48},{48,56},{56,64},{64,7... | collective-permute-start | bytes 663560 | tf_op jit(solution)/shard_map/ppermute | solution.py:298
  3.4 17.1 %collective-permute-start.1 = (bf16[216,512]{1,0:T(8,128)(2,1)S(1)}, bf16[216,512]{1,0:T(8,128)(2,1)S(1)}, u32[]{:S(2)}, u32[]{:S(2)}) collective-permute-start(bf16[216,512]{1,0:T(8,128)(2,1)S(1)} %get-tuple-element.24), channel_id=1, source_target_pairs={{8,0},{16,8},{24,16},{32,24},{40,32},{48,40},{56,48},{64,56},{72,6... | collective-permute-start | bytes 663560 | tf_op jit(solution)/shard_map/ppermute | solution.py:299
  20.6 8.8 %collective-permute-start.2 = (bf16[216,512]{1,0:T(8,128)(2,1)S(1)}, bf16[216,512]{1,0:T(8,128)(2,1)S(1)}, u32[]{:S(2)}, u32[]{:S(2)}) collective-permute-start(bf16[216,512]{1,0:T(8,128)(2,1)S(1)} %get-tuple-element.31), channel_id=1, source_target_pairs={{0,1},{1,0},{2,3},{3,2},{4,5},{5,4},{6,7},{7,6},{8,9},{9,8},{10,11... | collective-permute-start | bytes 663560 | tf_op jit(solution)/shard_map/ppermute | solution.py:306
  23.2 8.7 %collective-permute-start.3 = (bf16[216,512]{1,0:T(8,128)(2,1)S(1)}, bf16[216,512]{1,0:T(8,128)(2,1)S(1)}, u32[]{:S(2)}, u32[]{:S(2)}) collective-permute-start(bf16[216,512]{1,0:T(8,128)(2,1)S(1)} %get-tuple-element.33), channel_id=1, source_target_pairs={{1,2},{2,1},{3,4},{4,3},{5,6},{6,5},{9,10},{10,9},{11,12},{12,11},... | collective-permute-start | bytes 663560 | tf_op jit(solution)/shard_map/ppermute | solution.py:307
  27.7 1.7 %copy-start.4 = (s32[288]{0:T(512)S(1)}, s32[288]{0:T(512)}, u32[]{:S(2)}) copy-start(s32[288]{0:T(512)} %mask.1) | copy-start | bytes 3460

commit v7 on v5

--- a/solution.py
+++ b/solution.py
@@ -127,9 +127,8 @@
 
 
 def middle(x, gain, w_qkv, w_out, out, x32, stack, normed, q_rows, pairs, queries, context, mixed):
-    x32[...] = x[SHIFT : LAT - SHIFT].astype(F32)
     for lat in range(24):
-        stack[12 * lat : 12 * lat + 12, :] = x32[lat, 6:18, :]
+        stack[12 * lat : 12 * lat + 12, :] = x[SHIFT + lat].astype(F32)[6:18]
     attend(stack, gain, w_qkv, w_out, KEYS, normed, q_rows, pairs, queries, context, mixed)
     for lat in range(24):
         x32[lat, 6:18, :] = mixed[12 * lat : 12 * lat + 12, :]
@@ -138,12 +137,11 @@
 
 def side_windows(east, x, halo, done, gain, w_qkv, w_out, out, x32, halo32, stack, normed, q_rows, pairs, queries, context, mixed):
     lon = LON - SHIFT if east else 0
-    x32[...] = x[SHIFT : LAT - SHIFT].astype(F32)
     halo32[...] = halo[...].astype(F32)
     for band in range(2):
         base = KEYS * band
         for step in range(12):
-            stack[base + 6 * step : base + 6 * step + 6, :] = x32[12 * band + step, lon : lon + 6, :]
+            stack[base + 6 * step : base + 6 * step + 6, :] = x[SHIFT + 12 * band + step].astype(F32)[lon : lon + 6]
         stack[base + 72 : base + 144, :] = halo32[36 + 72 * band : 108 + 72 * band, :]
     attend(stack, gain, w_qkv, w_out, HALF, normed, q_rows, pairs, queries, context, mixed)
     x32[...] = done[...].astype(F32)

time: 35 us -> 34.9 us (level)
  no operation moved by 1% of the time
where the time goes in v7:
time: 34.9 us; the launch traced here: 34.7 us
  starting transfers between devices  21.3 us (61%)
  Pallas kernels  11.6 us (33%)
  local copies, waits for them, and re-layouts  1.18 us (3%)
  waiting for transfers between devices  0.44 us (1%)
    ppermute x1, starting transfers between devices, shards(): from_east = lax.ppermute(west, 'lon', [(b, a) for a, b in eastward])  13.5 us
    pallas_call x8, Pallas kernels, call(): pl.pallas_call(body, out_shape=out_shape, in_specs=specs, out_specs=jax.t...  11.6 us
    ppermute x1, starting transfers between devices, shards(): lax.ppermute(second, 'lat', [pair for a, b in northward[1::2] for pair in...  3.22 us
    ppermute x1, starting transfers between devices, shards(): lax.ppermute(first, 'lat', [pair for a, b in northward[0::2] for pair in...  2.58 us
    ppermute x1, starting transfers between devices, shards(): from_west = lax.ppermute(east, 'lon', eastward)  2.05 us
    unnamed x10, local copies, waits for them, and re-layouts  1.18 us
  transfers between devices with their start and end apart: 4, of which 1 were waited for; matrix products, arithmetic and copies ran while one was open for 0% of the time, Pallas kernels for 25%

profile of v7, /device:TPU:2, one launch (start us, length us, event | category | flops | bytes accessed | tf_op | source)
XLA Modules:
  0.0 34.7 jit_solution(11581307626152676991)
XLA Ops:
  0.0 0.0 copy-start.1
  0.0 1.2 %copy-done.1 = bf16[24,36,512]{2,0,1:T(8,128)(2,1)S(1)} copy-done((bf16[24,36,512]{2,0,1:T(8,128)(2,1)S(1)}, bf16[24,36,512]{2,0,1:T(8,128)(2,1)}, u32[]{:S(2)}) %copy-start.1) | copy-done | bytes 884760
  1.2 0.0 copy-start
  1.2 0.0 copy-start.2
  1.2 0.0 copy-start.3
  1.2 0.1 shard_map.56
  1.3 2.1 %collective-permute-start = (bf16[216,512]{1,0:T(8,128)(2,1)S(1)}, bf16[216,512]{1,0:T(8,128)(2,1)S(1)}, u32[]{:S(2)}, u32[]{:S(2)}) collective-permute-start(bf16[216,512]{1,0:T(8,128)(2,1)S(1)} %get-tuple-element.21), channel_id=1, source_target_pairs={{0,8},{8,16},{16,24},{24,32},{32,40},{40,48},{48,56},{56,64},{64,7... | collective-permute-start | bytes 663560 | tf_op jit(solution)/shard_map/ppermute | solution.py:307
  3.4 13.5 %collective-permute-start.1 = (bf16[216,512]{1,0:T(8,128)(2,1)S(1)}, bf16[216,512]{1,0:T(8,128)(2,1)S(1)}, u32[]{:S(2)}, u32[]{:S(2)}) collective-permute-start(bf16[216,512]{1,0:T(8,128)(2,1)S(1)} %get-tuple-element.24), channel_id=1, source_target_pairs={{8,0},{16,8},{24,16},{32,24},{40,32},{48,40},{56,48},{64,56},{72,6... | collective-permute-start | bytes 663560 | tf_op jit(solution)/shard_map/ppermute | solution.py:308
  16.9 0.0 copy-done
  16.9 0.0 copy-done.2
  16.9 0.0 copy-done.3
  16.9 2.0 %shard_map.55.refs_2_ = bf16[24,24,512]{2,1,0:T(8,128)(2,1)S(1)} custom-call(bf16[36,24,512]{2,1,0:T(8,128)(2,1)S(1)} %bitcast.4, f32[1,512]{1,0:T(1,128)S(1)} %bitcast.9, bf16[512,1536]{1,0:T(8,128)(2,1)S(1)} %copy-done, bf16[512,512]{1,0:T(8,128)(2,1)S(1)} %copy-done.2), custom_call_target="tpu_custom_call" | custom-call | flops 2000000000 | bytes 2000000 | tf_op jit(solution)/shard_map/pallas_call | solution.py:284
  18.9 0.0 collective-permute-done.refs_1_.from_west
  18.9 1.6 %shard_map.57.refs_2_ = bf16[24,24,512]{2,1,0:T(8,128)(2,1)S(1)} custom-call(bf16[36,24,512]{2,1,0:T(8,128)(2,1)S(1)} %bitcast.5, bf16[216,512]{1,0:T(8,128)(2,1)S(1)} %collective-permute-done.refs_1_.from_west, bf16[24,24,512]{2,1,0:T(8,128)(2,1)S(1)} %shard_map.55.refs_2_, f32[1,512]{1,0:T(1,128)S(1)} %bitcast.10, bf16[512,1536]{1,0:T(8,128)(2,1)S(1)} %copy-done, ...), custom_call_target="tpu_custom_call" | custom-call | flops 1000000 | bytes 1000 | tf_op jit(solution)/shard_map/pallas_call | solution.py:284
  20.5 0.0 collective-permute-done.1.from_east.refs_1_
  20.5 0.1 shard_map.60
  20.6 2.6 %collective-permute-start.2 = (bf16[216,512]{1,0:T(8,128)(2,1)S(1)}, bf16[216,512]{1,0:T(8,128)(2,1)S(1)}, u32[]{:S(2)}, u32[]{:S(2)}) collective-permute-start(bf16[216,512]{1,0:T(8,128)(2,1)S(1)} %get-tuple-element.31), channel_id=1, source_target_pairs={{0,1},{1,0},{2,3},{3,2},{4,5},{5,4},{6,7},{7,6},{8,9},{9,8},{10,11... | collective-permute-start | bytes 663560 | tf_op jit(solution)/shard_map/ppermute | solution.py:315
  23.2 3.2 %collective-permute-start.3 = (bf16[216,512]{1,0:T(8,128)(2,1)S(1)}, bf16[216,512]{1,0:T(8,128)(2,1)S(1)}, u32[]{:S(2)}, u32[]{:S(2)}) collective-permute-start(bf16[216,512]{1,0:T(8,128)(2,1)S(1)} %get-tuple-element.33), channel_id=1, source_target_pairs={{1,2},{2,1},{3,4},{4,3},{5,6},{6,5},{9,10},{10,9},{11,12},{12,11},... | collective-permute-start | bytes 663560 | tf_op jit(solution)/shard_map/ppermute | solution.py:316
  26.4 1.3 %shard_map.58 = (bf16[480,512]{1,0:T(8,128)(2,1)S(1)}, bf16[480,512]{1,0:T(8,128)(2,1)S(1)}, bf16[480,1024]{1,0:T(8,128)(2,1)S(1)}) custom-call(bf16[36,24,512]{2,1,0:T(8,128)(2,1)S(1)} %bitcast.7, bf16[216,512]{1,0:T(8,128)(2,1)S(1)} %collective-permute-done.refs_1_.from_west, bf16[216,512]{1,0:T(8,128)(2,1)S(1)} %collective-permute-done.1.from_east.refs_1_, ...), custom_call_target="tpu_custom_call" | custom-call | flops 1000000 | bytes 1000 | tf_op jit(solution)/shard_map/pallas_call | solution.py:284
  27.7 0.0 copy-start.4
  27.7 1.6 %shard_map.59.inner = bf16[24,24,512]{2,1,0:T(8,128)(2,1)S(1)} custom-call(bf16[36,24,512]{2,1,0:T(8,128)(2,1)S(1)} %bitcast.8, bf16[216,512]{1,0:T(8,128)(2,1)S(1)} %collective-permute-done.1.from_east.refs_1_, bf16[24,24,512]{2,1,0:T(8,128)(2,1)S(1)} %shard_map.57.refs_2_, f32[1,512]{1,0:T(1,128)S(1)} %bitcast.12, bf16[512,1536]{1,0:T(8,128)(2,1)S(1)} %copy-done, ...), custom_call_target="tpu_custom_call" | custom-call | flops 1000000 | bytes 1000 | tf_op jit(solution)/shard_map/pallas_call | solution.py:284
  29.3 0.0 collective-permute-done.2.refs_4_
  29.3 0.0 copy-done.4
  29.4 2.1 %shard_map.61.early = bf16[6,24,512]{2,1,0:T(8,128)(2,1)S(1)} custom-call(s32[288]{0:T(512)S(1)} %copy-done.4, bf16[480,512]{1,0:T(8,128)(2,1)S(1)} %get-tuple-element.27.refs_1_.raw, bf16[480,512]{1,0:T(8,128)(2,1)S(1)} %get-tuple-element.28.refs_2_.queries, bf16[480,1024]{1,0:T(8,128)(2,1)S(1)} %get-tuple-element.29.refs_3_.own_pairs, ...), custom_call_target="tpu_custom_call" | custom-call | flops 1000000 | bytes 1000 | tf_op jit(solution)/shard_map/pallas_call | solution.py:284
  31.5 0.4 %collective-permute-done.3.arrived = bf16[216,512]{1,0:T(8,128)(2,1)S(1)} collective-permute-done((bf16[216,512]{1,0:T(8,128)(2,1)S(1)}, bf16[216,512]{1,0:T(8,128)(2,1)S(1)}, u32[]{:S(2)}, u32[]{:S(2)}) %collective-permute-start.3) | collective-permute-done | bytes 221216 | tf_op jit(solution)/shard_map/ppermute | solution.py:316
  31.9 2.8 %shard_map.62 = bf16[36,24,512]{2,1,0:T(8,128)(2,1)} custom-call(s32[288]{0:T(512)S(1)} %copy-done.4, bf16[480,512]{1,0:T(8,128)(2,1)S(1)} %get-tuple-element.27.refs_1_.raw, bf16[480,512]{1,0:T(8,128)(2,1)S(1)} %get-tuple-element.28.refs_2_.queries, bf16[480,1024]{1,0:T(8,128)(2,1)S(1)} %get-tuple-element.29.refs_3_.own_pairs, ...), custom_call_target="tpu_custom_call" | custom-call | flops 2000000000 | bytes 2000000 | tf_op jit(solution)/shard_map/pallas_call | solution.py:284
Async XLA Ops:
  0.0 1.2 %copy-start.1 = (bf16[24,36,512]{2,0,1:T(8,128)(2,1)S(1)}, bf16[24,36,512]{2,0,1:T(8,128)(2,1)}, u32[]{:S(2)}) copy-start(bf16[24,36,512]{2,0,1:T(8,128)(2,1)} %param.5) | copy-start | bytes 2654212
  1.2 15.7 %copy-start = (bf16[512,1536]{1,0:T(8,128)(2,1)S(1)}, bf16[512,1536]{1,0:T(8,128)(2,1)}, u32[]{:S(2)}) copy-start(bf16[512,1536]{1,0:T(8,128)(2,1)} %w_qkv.5) | copy-start | bytes 4718596
  1.2 15.7 %copy-start.2 = (bf16[512,512]{1,0:T(8,128)(2,1)S(1)}, bf16[512,512]{1,0:T(8,128)(2,1)}, u32[]{:S(2)}) copy-start(bf16[512,512]{1,0:T(8,128)(2,1)} %w_out.3) | copy-start | bytes 1572868
  1.2 15.7 %copy-start.3 = (f32[512]{0:T(512)S(1)}, f32[512]{0:T(512)}, u32[]{:S(2)}) copy-start(f32[512]{0:T(512)} %param.6) | copy-start | bytes 6148
  1.3 17.5 %collective-permute-start = (bf16[216,512]{1,0:T(8,128)(2,1)S(1)}, bf16[216,512]{1,0:T(8,128)(2,1)S(1)}, u32[]{:S(2)}, u32[]{:S(2)}) collective-permute-start(bf16[216,512]{1,0:T(8,128)(2,1)S(1)} %get-tuple-element.21), channel_id=1, source_target_pairs={{0,8},{8,16},{16,24},{24,32},{32,40},{40,48},{48,56},{56,64},{64,7... | collective-permute-start | bytes 663560 | tf_op jit(solution)/shard_map/ppermute | solution.py:307
  3.4 17.1 %collective-permute-start.1 = (bf16[216,512]{1,0:T(8,128)(2,1)S(1)}, bf16[216,512]{1,0:T(8,128)(2,1)S(1)}, u32[]{:S(2)}, u32[]{:S(2)}) collective-permute-start(bf16[216,512]{1,0:T(8,128)(2,1)S(1)} %get-tuple-element.24), channel_id=1, source_target_pairs={{8,0},{16,8},{24,16},{32,24},{40,32},{48,40},{56,48},{64,56},{72,6... | collective-permute-start | bytes 663560 | tf_op jit(solution)/shard_map/ppermute | solution.py:308
  20.6 8.8 %collective-permute-start.2 = (bf16[216,512]{1,0:T(8,128)(2,1)S(1)}, bf16[216,512]{1,0:T(8,128)(2,1)S(1)}, u32[]{:S(2)}, u32[]{:S(2)}) collective-permute-start(bf16[216,512]{1,0:T(8,128)(2,1)S(1)} %get-tuple-element.31), channel_id=1, source_target_pairs={{0,1},{1,0},{2,3},{3,2},{4,5},{5,4},{6,7},{7,6},{8,9},{9,8},{10,11... | collective-permute-start | bytes 663560 | tf_op jit(solution)/shard_map/ppermute | solution.py:315
  23.2 8.7 %collective-permute-start.3 = (bf16[216,512]{1,0:T(8,128)(2,1)S(1)}, bf16[216,512]{1,0:T(8,128)(2,1)S(1)}, u32[]{:S(2)}, u32[]{:S(2)}) collective-permute-start(bf16[216,512]{1,0:T(8,128)(2,1)S(1)} %get-tuple-element.33), channel_id=1, source_target_pairs={{1,2},{2,1},{3,4},{4,3},{5,6},{6,5},{9,10},{10,9},{11,12},{12,11},... | collective-permute-start | bytes 663560 | tf_op jit(solution)/shard_map/ppermute | solution.py:316
  27.7 1.7 %copy-start.4 = (s32[288]{0:T(512)S(1)}, s32[288]{0:T(512)}, u32[]{:S(2)}) copy-start(s32[288]{0:T(512)} %mask.1) | copy-start | bytes 3460
